TPU v7x, 32 devices: a whole 2x2x4 slice. The times are simulated.
32 devices in a mesh: chan: 8 (over z, core), rec: 4 (over y, x).
Axes of the slice: x: 2, y: 2, z: 4, core: 2. Of those that a mesh axis runs over, the one named last changes fastest.
Arguments:
- strain_rate: bfloat16 [16, 4096, 2048], P('rec', 'chan'), may hold values from -6 to 6
Outputs:
- stacked_cross: float32 [4096, 8192], P(('chan', 'rec'))
All inputs are finite; a program needn't handle non-finite values.
Results may differ from a plain program's by a relative error of at most 0.003.
Values sent between devices are 32-bit elements; how exact they have to be, the bound alone decides.
No kernel may reach another device: no remote copies, remote signals or barrier semaphores. Data moves between devices by JAX's collectives and lax.ppermute only.
A program may use at most 128 MiB of HBM per device.

v0:
```python
import math

import jax
import jax.numpy as jnp
from jax import lax
from jax.sharding import PartitionSpec as P

S = 2048
F = 64
K = 64
BIN0 = 32


def shifted(shard, axis, by):
    length = lax.axis_size(axis)
    pairs = [(i, i + by) for i in range(length) if 0 <= i + by < length]
    return lax.ppermute(shard, axis, pairs)


def make_tables():
    sample_idx = jnp.arange(S, dtype=jnp.int32)
    bin_idx = BIN0 + jnp.arange(F, dtype=jnp.int32)
    phase = sample_idx[:, None] * bin_idx[None, :] % S
    angle = 2.0 * math.pi / S * phase.astype(jnp.float32)
    return (jnp.cos(angle).astype(jnp.bfloat16), jnp.sin(angle).astype(jnp.bfloat16))


def whiten(block, cos_table, sin_table):
    spec_re = jnp.dot(block, cos_table, preferred_element_type=jnp.float32)
    spec_im = -jnp.dot(block, sin_table, preferred_element_type=jnp.float32)
    power = jnp.mean(spec_re * spec_re + spec_im * spec_im, axis=-1, keepdims=True)
    scale = 1.0 / jnp.sqrt(power + 1e-06)
    return jnp.concatenate([spec_re * scale, spec_im * scale], axis=-1)


def record_sum(own_all, ext_all, count):
    a_re = own_all[:, :, :F]
    a_im = own_all[:, :, F:]
    columns = []
    for offset in range(K):
        partner = ext_all[:, offset : offset + count, :]
        b_re = partner[:, :, :F]
        b_im = partner[:, :, F:]
        cross_re = jnp.sum(a_re * b_re + a_im * b_im, axis=0)
        cross_im = jnp.sum(a_im * b_re - a_re * b_im, axis=0)
        columns.append(jnp.concatenate([cross_re, cross_im], axis=-1))
    return jnp.concatenate(columns, axis=1)


def per_device(strain_rate):
    cos_table, sin_table = make_tables()
    whitened = whiten(strain_rate, cos_table, sin_table)
    ch_local = whitened.shape[1]
    rec_devs = lax.axis_size("rec")
    records = whitened.shape[0] * rec_devs
    rows_out = ch_local // rec_devs
    below = shifted(whitened[:, : K - 1, :], "chan", -1)
    extended = jnp.concatenate([whitened, below], axis=1)
    summed = lax.psum_scatter(
        record_sum(whitened, extended, rows_out * lax.axis_size("rec")),
        "rec",
        scatter_dimension=0,
        tiled=True,
    )
    return summed / records


def solution(mesh):
    placed = (P("rec", "chan", None),)
    return jax.shard_map(
        per_device, mesh=mesh, in_specs=placed, out_specs=P(("chan", "rec"), None), check_vma=False
    )
```

profile of v0, /device:TPU:0, one launch (start us, length us, event | category | flops | bytes accessed | tf_op | source)
XLA Modules:
  0.0 304.0 jit_solution(8902730501414884470)
XLA Ops:
  6.5 6.5 %fusion.7 = f32[64,4,512]{2,0,1:T(8,128)S(1)} fusion(bf16[4,512,2048]{2,1,0:T(8,128)(2,1)} %param.1, s32[64]{0:T(128)S(1)} %iota_add_fusion), kind=kOutput, calls=%fused_computation.273 | convolution fusion | flops 538836992 | bytes 8913152 | tf_op jit(solution)/shard_map/dot_general | solution.py:29
  13.1 6.7 %add_reduce_fusion.64 = (f32[4,512]{1,0:T(4,128)S(1)}, f32[64,4,512]{2,0,1:T(8,128)S(1)}) fusion(f32[64,4,512]{2,0,1:T(8,128)S(1)} %fusion.7, bf16[4,512,2048]{2,1,0:T(8,128)(2,1)} %param.1, s32[64]{0:T(128)S(1)} %iota_add_fusion), kind=kOutput, calls=%fused_computation.138 | convolution fusion | flops 539359232 | bytes 9445632 | tf_op jit(solution)/shard_map/dot_general | solution.py:30
  19.9 1.5 collective-permute-start
  21.4 1.9 collective-permute-done
  23.5 2.6 subtract_reduce_fusion.12
  26.0 2.2 subtract_reduce_fusion.28
  28.2 2.5 subtract_reduce_fusion.8
  30.7 2.5 subtract_reduce_fusion.40
  33.2 2.5 subtract_reduce_fusion.4
  35.7 2.5 subtract_reduce_fusion.24
  38.2 2.5 subtract_reduce_fusion.16
  40.7 2.7 subtract_reduce_fusion.20
  44.1 0.7 constant_dynamic-update-slice_fusion.126
  44.8 0.7 constant_dynamic-update-slice_fusion.125
  46.1 0.7 constant_dynamic-update-slice_fusion.123
  48.1 0.7 constant_dynamic-update-slice_fusion.120
  49.4 0.7 constant_dynamic-update-slice_fusion.118
  50.7 0.7 constant_dynamic-update-slice_fusion.116
  53.3 0.7 constant_dynamic-update-slice_fusion.112
  54.0 0.7 constant_dynamic-update-slice_fusion.111
  56.0 0.7 constant_dynamic-update-slice_fusion.108
  57.3 0.7 constant_dynamic-update-slice_fusion.106
  58.6 0.7 constant_dynamic-update-slice_fusion.104
  60.6 0.7 constant_dynamic-update-slice_fusion.101
  63.8 0.7 constant_dynamic-update-slice_fusion.96
  66.4 0.7 constant_dynamic-update-slice_fusion.92
  67.1 0.7 constant_dynamic-update-slice_fusion.91
  69.1 0.7 constant_dynamic-update-slice_fusion.88
  70.4 0.7 constant_dynamic-update-slice_fusion.86
  71.1 0.7 constant_dynamic-update-slice_fusion.85
  71.7 0.7 constant_dynamic-update-slice_fusion.84
  72.4 0.7 constant_dynamic-update-slice_fusion.83
  73.0 0.7 constant_dynamic-update-slice_fusion.82
  73.7 0.7 constant_dynamic-update-slice_fusion.81
  79.6 0.7 constant_dynamic-update-slice_fusion.72
  84.9 0.7 constant_dynamic-update-slice_fusion.64
  85.5 0.7 constant_dynamic-update-slice_fusion.63
  88.2 0.7 constant_dynamic-update-slice_fusion.59
  88.8 0.7 constant_dynamic-update-slice_fusion.58
  89.5 0.7 constant_dynamic-update-slice_fusion.57
  90.1 0.7 constant_dynamic-update-slice_fusion.56
  92.8 0.7 constant_dynamic-update-slice_fusion.52
  94.1 0.7 constant_dynamic-update-slice_fusion.50
  95.4 0.7 constant_dynamic-update-slice_fusion.48
  97.4 0.7 constant_dynamic-update-slice_fusion.45
  98.0 0.7 constant_dynamic-update-slice_fusion.44
  98.7 0.7 constant_dynamic-update-slice_fusion.43
  99.4 0.7 constant_dynamic-update-slice_fusion.42
  105.9 0.7 constant_dynamic-update-slice_fusion.32
  106.6 0.7 constant_dynamic-update-slice_fusion.31
  109.2 0.7 constant_dynamic-update-slice_fusion.27
  109.9 0.7 constant_dynamic-update-slice_fusion.26
  111.9 0.7 constant_dynamic-update-slice_fusion.23
  112.5 0.7 constant_dynamic-update-slice_fusion.22
  116.4 0.7 constant_dynamic-update-slice_fusion.16
  117.8 0.7 constant_dynamic-update-slice_fusion.14
  119.1 0.7 constant_dynamic-update-slice_fusion.12
  120.4 0.7 constant_dynamic-update-slice_fusion.10
  121.7 0.7 constant_dynamic-update-slice_fusion.8
  123.7 0.7 constant_dynamic-update-slice_fusion.5
  127.0 0.7 constant_dynamic-update-slice_fusion
  127.6 159.5 %reduce-scatter.2.cloned.1.call-done = f32[128,8192]{0,1:T(8,128)} async-done(((f32[512,8192]{0,1:T(8,128)}), f32[128,8192]{0,1:T(8,128)}) %reduce-scatter.2.cloned.1.call-update) | async-done | bytes 4194320 | tf_op jit(solution)/shard_map/reduce_scatter | solution.py:59
  287.2 4.4 %broadcast_multiply_fusion = f32[128,8192]{0,1:T(8,128)} fusion(f32[128,8192]{0,1:T(8,128)} %reduce-scatter.2.cloned.1.call-done), kind=kLoop, calls=%fused_computation | loop fusion | flops 1048576 | bytes 8388608 | tf_op jit(solution)/shard_map/div | solution.py:65
  291.5 5.6 %copy.2 = f32[128,8192]{1,0:T(8,128)} copy(f32[128,8192]{0,1:T(8,128)} %broadcast_multiply_fusion) | data formatting | bytes 8388608 | tf_op jit(solution)/shard_map/div | solution.py:65
  (86 shorter events, 51.9 us)
Async XLA Ops:
  6.5 280.6 %reduce-scatter.2.cloned.1.call-start = ((), (), s32[]{:S(2)}) async-start(), calls=%async_computation.1 | async-start | bytes 20971520 | tf_op jit(solution)/shard_map/reduce_scatter | solution.py:59
  19.9 3.4 %collective-permute-start = (f32[4,63,128]{1,2,0:T(8,128)S(1)}, f32[4,63,128]{1,2,0:T(8,128)S(1)}, u32[]{:S(2)}, u32[]{:S(2)}) collective-permute-start(f32[4,63,128]{1,2,0:T(8,128)S(1)} %pad_maximum_fusion.1), channel_id=1, source_target_pairs={{4,0},{8,4},{12,8},{16,12},{20,16},{24,20},{28,24},{5,1},{9,5},{13... | collective-permute-start | bytes 387080 | tf_op jit(solution)/shard_map/ppermute | solution.py:17
Sparse Core Ops, SparseCore 0:
  127.8 159.3 reduce-scatter.1
where the time goes:
time: 304 us
  waiting for transfers between devices  161 us (53%)
  local copies, waits for them, and re-layouts  89.7 us (30%)
  other arithmetic  24.6 us (8%)
  between operations  13.6 us (4%)
  matrix products  13.2 us (4%)
    reduce_scatter x1, waiting for transfers between devices, per_device(): lax.psum_scatter(record_sum(whitened, extended, rows_out * lax.axis_size(...  160 us
    unnamed x127, local copies, waits for them, and re-layouts  83.4 us
    reduce_sum x8, other arithmetic, record_sum(): cross_im = jnp.sum(a_im * b_re - a_re * b_im, axis=0)  19.9 us
    dot_general x1, matrix products, whiten(): spec_im = -jnp.dot(block, sin_table, preferred_element_type=jnp.float32)  6.66 us
    dot_general x1, matrix products, whiten(): spec_re = jnp.dot(block, cos_table, preferred_element_type=jnp.float32)  6.51 us
  transfers between devices with their start and end apart: 2, of which 2 were waited for; matrix products, arithmetic and copies ran while one was open for 0% of the time, Pallas kernels for 0%

commit v1 on v0

v1 whole, which is shorter than its diff:
```python
import functools
import math

import jax
import jax.numpy as jnp
import numpy as np
from jax import lax
from jax.experimental import pallas as pl
from jax.experimental.pallas import tpu as pltpu
from jax.sharding import PartitionSpec as P

S = 2048
F = 64
K = 64
BIN0 = 32
W = 2 * F
SUB = 8


def make_table():
    phase = np.arange(S)[:, None] * (BIN0 + np.arange(F))[None, :] % S
    angle = 2.0 * math.pi / S * phase
    return np.concatenate([np.cos(angle), -np.sin(angle)], axis=1).astype(jnp.bfloat16)


def whiten_kernel(pos_ref, table_ref, *refs):
    count = len(refs) // 2
    for strain_ref, out_ref in zip(refs[:count], refs[count:]):
        spec = jnp.dot(strain_ref[0], table_ref[...], preferred_element_type=jnp.float32)
        power = jnp.sum(spec * spec, axis=-1, keepdims=True) * (1.0 / F)
        out_ref[0] = spec * lax.rsqrt(power + 1e-06)


def whiten(strain, table, pos, pick, rows):
    records, _, samples = strain.shape

    def in_spec(i):
        return pl.BlockSpec((1, rows, samples), lambda r, p: (r, p[i], 0))

    out = jax.ShapeDtypeStruct((records, rows, W), jnp.float32)
    return pl.pallas_call(
        whiten_kernel,
        out_shape=[out] * len(pick),
        grid_spec=pltpu.PrefetchScalarGridSpec(
            num_scalar_prefetch=1,
            grid=(records,),
            in_specs=[pl.BlockSpec((samples, W), lambda r, p: (0, 0))] + [in_spec(i) for i in pick],
            out_specs=[pl.BlockSpec((1, rows, W), lambda r, p: (r, 0, 0))] * len(pick),
        ),
        compiler_params=pltpu.CompilerParams(vmem_limit_bytes=24 * 2**20),
        cost_estimate=pl.CostEstimate(
            flops=2 * records * rows * samples * W * len(pick),
            bytes_accessed=2 * records * rows * samples * len(pick),
            transcendentals=0,
        ),
        name="whiten",
    )(pos, table, *([strain] * len(pick)))


def cross_kernel(scale, groups, k_range, has_acc, refs_per_group, *refs):
    refs = list(refs)
    acc_ref = refs.pop(0) if has_acc else None
    ins = [[refs.pop(0) for _ in range(n)] for n in refs_per_group]
    out_ref, a_ref, b_ref = refs
    t = pl.program_id(0)

    @pl.when(t == 0)
    def _():
        lane = lax.broadcasted_iota(jnp.int32, (1, W), 1)
        low = lane < F
        g = 0
        for parts in ins:
            n = parts[0].shape[0]
            for r in range(n):
                at = 0
                for i, part in enumerate(parts):
                    rows = part.shape[1]
                    w = part[r]
                    turned = pltpu.roll(w, F, 1)
                    b_ref[0, g, at : at + rows] = jnp.where(low, w, turned)
                    b_ref[1, g, at : at + rows] = jnp.where(low, turned, w)
                    if i == 0:
                        own = a_ref.shape[2]
                        a_ref[0, g] = w[:own] * scale
                        a_ref[1, g] = (jnp.where(low, turned, -turned))[:own] * scale
                    at += rows
                g += 1

    first, last, tile = k_range(t)
    row0 = tile * SUB
    left = [
        (a_ref[0, g, pl.ds(row0, SUB)], a_ref[1, g, pl.ds(row0, SUB)]) for g in range(groups)
    ]

    def step(q, carry):
        for u in range(SUB):
            k = q * SUB + u
            total = acc_ref[:, pl.ds(k * W, W)] if has_acc else None
            for g in range(groups):
                term = left[g][0] * b_ref[0, g, pl.ds(row0 + k, SUB)]
                total = term if total is None else total + term
                total = total + left[g][1] * b_ref[1, g, pl.ds(row0 + k, SUB)]
            out_ref[:, pl.ds(k * W, W)] = total
        return carry

    lax.fori_loop(first, last, step, 0)


def cross(groups_in, rows, scale, acc=None, region="all"):
    tiles = rows // SUB
    steps = K // SUB
    tile0 = 0
    if region == "all":
        k_range = lambda t: (0, steps, t)
    elif region == "main":
        k_range = lambda t: (0, jnp.minimum(steps, tiles - 1 - t), t)
    else:
        tile0 = tiles - steps
        tiles = steps
        k_range = lambda t: (steps - 1 - t, steps, t + tile0)
    records = sum(g[0].shape[0] for g in groups_in)
    ext = max(sum(p.shape[1] for p in g) for g in groups_in)
    flat = [p for g in groups_in for p in g]
    whole = [pl.BlockSpec(p.shape, lambda t: (0, 0, 0)) for p in flat]
    block = pl.BlockSpec((SUB, K * W), lambda t: (t + tile0, 0))
    return pl.pallas_call(
        functools.partial(
            cross_kernel, scale, records, k_range, acc is not None, [len(g) for g in groups_in]
        ),
        out_shape=jax.ShapeDtypeStruct((rows, K * W), jnp.float32),
        grid=(tiles,),
        in_specs=([block] if acc is not None else []) + whole,
        out_specs=block,
        scratch_shapes=[
            pltpu.VMEM((2, records, rows, W), jnp.float32),
            pltpu.VMEM((2, records, ext, W), jnp.float32),
        ],
        input_output_aliases={0: 0} if acc is not None else {},
        compiler_params=pltpu.CompilerParams(vmem_limit_bytes=32 * 2**20),
        cost_estimate=pl.CostEstimate(
            flops=8 * records * rows * K * W, bytes_accessed=4 * rows * K * W, transcendentals=0
        ),
        name="cross_" + region,
    )(*([acc] if acc is not None else []), *flat)


def xor_pairs(size, by):
    return [(i, i ^ by) for i in range(size)]


def shifted(shard, axis, by):
    length = lax.axis_size(axis)
    pairs = [(i, i + by) for i in range(length) if 0 <= i + by < length]
    return lax.ppermute(shard, axis, pairs)


def per_device(strain):
    table = jnp.asarray(make_table())
    records, channels, _ = strain.shape
    size = lax.axis_size("rec")
    rows = channels // size
    scale = 1.0 / (records * size)
    zero = jnp.zeros((1,), jnp.int32)
    me = lax.axis_index("rec")

    (spectra,) = whiten(strain, table, zero, [0], channels)
    below = shifted(spectra[:, :K], "chan", -1)
    extended = jnp.concatenate([spectra, below], axis=1)
    pieces = []
    for by in range(size):
        part = lax.dynamic_slice_in_dim(extended, (me ^ by) * rows, rows + K, 1)
        pieces.append(lax.ppermute(part, "rec", xor_pairs(size, by)) if by else part)
    return cross([[p] for p in pieces], rows, scale)


def solution(mesh):
    placed = (P("rec", "chan", None),)
    return jax.shard_map(
        per_device, mesh=mesh, in_specs=placed, out_specs=P(("chan", "rec"), None), check_vma=False
    )
```

time: 304 us -> 55.5 us (0.18)
  waiting for transfers between devices: 161 us -> 19.6 us
  local copies, waits for them, and re-layouts: 89.7 us -> 4.43 us
  Pallas kernels: 0 us -> 24.5 us
  other arithmetic: 24.6 us -> 0.27 us
  between operations: 13.6 us -> 0.06 us
  matrix products: 13.2 us -> 0 us
  starting transfers between devices: 1.47 us -> 5.88 us
    reduce_scatter x1 -> x0, waiting for transfers between devices: 160 us -> none  [per_device(): lax.psum_scatter(record_sum(whitened, extended, rows_out * lax.axis_size(...]
    unnamed x127 -> x4, local copies, waits for them, and re-layouts: 83.4 us -> 4.42 us
    pallas_call x0 -> x2, Pallas kernels: none -> 24.5 us  [the longest x1 21.3 us: cross(): pl.pallas_call(functools.partial(cross_kernel, scale, records, k_range, a...]
    reduce_sum x8 -> x0, other arithmetic: 19.9 us -> none  [record_sum(): cross_im = jnp.sum(a_im * b_re - a_re * b_im, axis=0)]
    ppermute x0 -> x3, waiting for transfers between devices: none -> 17.7 us  [per_device(): lax.ppermute(part, 'rec', xor_pairs(size, by))]
    dot_general x2 -> x0, matrix products: 13.2 us -> none  [the longest x1 6.66 us: whiten(): spec_im = -jnp.dot(block, sin_table, preferred_element_type=jnp.float32)]
    div x1 -> x0, local copies, waits for them, and re-layouts: 5.59 us -> none  [per_device(): return summed / records]
    ppermute x0 -> x3, starting transfers between devices: none -> 4.59 us  [per_device(): lax.ppermute(part, 'rec', xor_pairs(size, by))]
  transfers between devices with their start and end apart: 2 -> 4, of which waited for: 2 -> 4; matrix products, arithmetic and copies ran while one was open for 0% -> 0% of each run, Pallas kernels for 0% -> 0%
where the time goes in v1:
time: 55.5 us; the launch traced here: 54.7 us
  Pallas kernels  24.5 us (44%)
  waiting for transfers between devices  19.6 us (35%)
  starting transfers between devices  5.88 us (11%)
  local copies, waits for them, and re-layouts  4.43 us (8%)
    pallas_call x1, Pallas kernels, cross(): pl.pallas_call(functools.partial(cross_kernel, scale, records, k_range, a...  21.3 us
    ppermute x3, waiting for transfers between devices, per_device(): lax.ppermute(part, 'rec', xor_pairs(size, by))  17.7 us
    ppermute x3, starting transfers between devices, per_device(): lax.ppermute(part, 'rec', xor_pairs(size, by))  4.59 us
    unnamed x4, local copies, waits for them, and re-layouts  4.42 us
    pallas_call x1, Pallas kernels, whiten(): pl.pallas_call(whiten_kernel, out_shape=[out] * len(pick), grid_spec=pltp...  3.21 us
    ppermute x1, waiting for transfers between devices, shifted(): return lax.ppermute(shard, axis, pairs)  1.92 us
    ppermute x1, starting transfers between devices, shifted(): return lax.ppermute(shard, axis, pairs)  1.29 us
  transfers between devices with their start and end apart: 4, of which 4 were waited for; matrix products, arithmetic and copies ran while one was open for 0% of the time, Pallas kernels for 0%

profile of v1, /device:TPU:0, one launch (start us, length us, event | category | flops | bytes accessed | tf_op | source)
XLA Modules:
  0.0 54.7 jit_solution(11895880298123787374)
XLA Ops:
  0.0 0.0 copy-start
  0.0 3.4 %copy-done = bf16[4,512,2048]{2,1,0:T(8,128)(2,1)S(1)} copy-done((bf16[4,512,2048]{2,1,0:T(8,128)(2,1)S(1)}, bf16[4,512,2048]{2,1,0:T(8,128)(2,1)}, u32[]{:S(2)}) %copy-start) | copy-done | bytes 8388632
  3.4 0.0 copy-start.1
  3.4 1.0 %copy-done.1 = bf16[2048,128]{1,0:T(8,128)(2,1)S(1)} copy-done((bf16[2048,128]{1,0:T(8,128)(2,1)S(1)}, bf16[2048,128]{1,0:T(8,128)(2,1)}, u32[]{:S(2)}) %copy-start.1) | copy-done | bytes 524312
  4.4 3.2 %whiten.1 = f32[4,512,128]{2,1,0:T(8,128)S(1)} custom-call(s32[1]{0:T(128)} %constant.9.clone.1.pos_ref, bf16[2048,128]{1,0:T(8,128)(2,1)S(1)} %copy-done.1, bf16[4,512,2048]{2,1,0:T(8,128)(2,1)S(1)} %copy-done), custom_call_target="tpu_custom_call" | custom-call | flops 1073741824 | bytes 8388608 | tf_op jit(solution)/shard_map/whiten/pallas_call | solution.py:41
  7.7 1.3 %collective-permute-start = (f32[4,64,128]{2,1,0:T(8,128)S(1)}, f32[4,64,128]{2,1,0:T(8,128)S(1)}, u32[]{:S(2)}, u32[]{:S(2)}) collective-permute-start(f32[4,64,128]{2,1,0:T(8,128)S(1)} %slice.4), channel_id=1, source_target_pairs={{4,0},{8,4},{12,8},{16,12},{20,16},{24,20},{28,24},{5,1},{9,5},{13... | collective-permute-start | bytes 393224 | tf_op jit(solution)/shard_map/ppermute | solution.py:154
  9.0 1.9 %collective-permute-done = f32[4,64,128]{2,1,0:T(8,128)S(1)} collective-permute-done((f32[4,64,128]{2,1,0:T(8,128)S(1)}, f32[4,64,128]{2,1,0:T(8,128)S(1)}, u32[]{:S(2)}, u32[]{:S(2)}) %collective-permute-start) | collective-permute-done | bytes 131104 | tf_op jit(solution)/shard_map/ppermute | solution.py:154
  10.9 0.3 fusion
  11.2 3.9 %collective-permute-start.3 = (f32[4,192,128]{2,1,0:T(8,128)S(1)}, f32[4,192,128]{2,1,0:T(8,128)S(1)}, u32[]{:S(2)}, u32[]{:S(2)}) collective-permute-start(f32[4,192,128]{2,1,0:T(8,128)S(1)} %get-tuple-element.5), channel_id=1, source_target_pairs={{0,3},{1,2},{2,1},{3,0},{4,7},{5,6},{6,5},{7,4},{8,11},{9,10},{10,... | collective-permute-start | bytes 1179656 | tf_op jit(solution)/shard_map/ppermute | solution.py:172
  15.1 0.5 collective-permute-start.1
  15.7 0.1 collective-permute-start.2
  15.8 6.9 %collective-permute-done.3.refs_3_ = f32[4,192,128]{2,1,0:T(8,128)S(1)} collective-permute-done((f32[4,192,128]{2,1,0:T(8,128)S(1)}, f32[4,192,128]{2,1,0:T(8,128)S(1)}, u32[]{:S(2)}, u32[]{:S(2)}) %collective-permute-start.3) | collective-permute-done | bytes 393248 | tf_op jit(solution)/shard_map/ppermute | solution.py:172
  22.6 9.4 %collective-permute-done.1.refs_1_ = f32[4,192,128]{2,1,0:T(8,128)S(1)} collective-permute-done((f32[4,192,128]{2,1,0:T(8,128)S(1)}, f32[4,192,128]{2,1,0:T(8,128)S(1)}, u32[]{:S(2)}, u32[]{:S(2)}) %collective-permute-start.1) | collective-permute-done | bytes 393248 | tf_op jit(solution)/shard_map/ppermute | solution.py:172
  32.0 1.4 %collective-permute-done.2.refs_2_ = f32[4,192,128]{2,1,0:T(8,128)S(1)} collective-permute-done((f32[4,192,128]{2,1,0:T(8,128)S(1)}, f32[4,192,128]{2,1,0:T(8,128)S(1)}, u32[]{:S(2)}, u32[]{:S(2)}) %collective-permute-start.2) | collective-permute-done | bytes 393248 | tf_op jit(solution)/shard_map/ppermute | solution.py:172
  33.4 21.3 %cross_all.1 = f32[128,8192]{1,0:T(8,128)} custom-call(f32[4,192,128]{2,1,0:T(8,128)S(1)} %get-tuple-element.6.refs_0_, f32[4,192,128]{2,1,0:T(8,128)S(1)} %collective-permute-done.1.refs_1_, f32[4,192,128]{2,1,0:T(8,128)S(1)} %collective-permute-done.2.refs_2_, f32[4,192,128]{2,1,0:T(8,128)S(1)} %collective-permute-done.3.refs_3_), custom_call_target="tpu_custom_call" | custom-call | flops 134217728 | bytes 4194304 | tf_op jit(solution)/shard_map/cross_all/pallas_call | solution.py:126
  (1 shorter events, 0.0 us)
Async XLA Ops:
  0.0 3.4 %copy-start = (bf16[4,512,2048]{2,1,0:T(8,128)(2,1)S(1)}, bf16[4,512,2048]{2,1,0:T(8,128)(2,1)}, u32[]{:S(2)}) copy-start(bf16[4,512,2048]{2,1,0:T(8,128)(2,1)} %refs_0_.1) | copy-start | bytes 25165828
  3.4 1.0 %copy-start.1 = (bf16[2048,128]{1,0:T(8,128)(2,1)S(1)}, bf16[2048,128]{1,0:T(8,128)(2,1)}, u32[]{:S(2)}) copy-start(bf16[2048,128]{1,0:T(8,128)(2,1)} %constant.20.clone.table_ref) | copy-start | bytes 1572868
  7.7 3.2 %collective-permute-start = (f32[4,64,128]{2,1,0:T(8,128)S(1)}, f32[4,64,128]{2,1,0:T(8,128)S(1)}, u32[]{:S(2)}, u32[]{:S(2)}) collective-permute-start(f32[4,64,128]{2,1,0:T(8,128)S(1)} %slice.4), channel_id=1, source_target_pairs={{4,0},{8,4},{12,8},{16,12},{20,16},{24,20},{28,24},{5,1},{9,5},{13... | collective-permute-start | bytes 393224 | tf_op jit(solution)/shard_map/ppermute | solution.py:154
  11.2 11.4 %collective-permute-start.3 = (f32[4,192,128]{2,1,0:T(8,128)S(1)}, f32[4,192,128]{2,1,0:T(8,128)S(1)}, u32[]{:S(2)}, u32[]{:S(2)}) collective-permute-start(f32[4,192,128]{2,1,0:T(8,128)S(1)} %get-tuple-element.5), channel_id=1, source_target_pairs={{0,3},{1,2},{2,1},{3,0},{4,7},{5,6},{6,5},{7,4},{8,11},{9,10},{10,... | collective-permute-start | bytes 1179656 | tf_op jit(solution)/shard_map/ppermute | solution.py:172
  15.1 16.9 %collective-permute-start.1 = (f32[4,192,128]{2,1,0:T(8,128)S(1)}, f32[4,192,128]{2,1,0:T(8,128)S(1)}, u32[]{:S(2)}, u32[]{:S(2)}) collective-permute-start(f32[4,192,128]{2,1,0:T(8,128)S(1)} %get-tuple-element.7), channel_id=1, source_target_pairs={{0,1},{1,0},{2,3},{3,2},{4,5},{5,4},{6,7},{7,6},{8,9},{9,8},{10,11... | collective-permute-start | bytes 1179656 | tf_op jit(solution)/shard_map/ppermute | solution.py:172
  15.7 17.8 %collective-permute-start.2 = (f32[4,192,128]{2,1,0:T(8,128)S(1)}, f32[4,192,128]{2,1,0:T(8,128)S(1)}, u32[]{:S(2)}, u32[]{:S(2)}) collective-permute-start(f32[4,192,128]{2,1,0:T(8,128)S(1)} %get-tuple-element.8), channel_id=1, source_target_pairs={{0,2},{1,3},{2,0},{3,1},{4,6},{5,7},{6,4},{7,5},{8,10},{9,11},{10,... | collective-permute-start | bytes 1179656 | tf_op jit(solution)/shard_map/ppermute | solution.py:172

commit v2 on v0

v2 whole, which is shorter than its diff:
```python
import functools
import math

import jax
import jax.numpy as jnp
from jax import lax
from jax.experimental import pallas as pl
from jax.experimental.pallas import tpu as pltpu
from jax.sharding import PartitionSpec as P

S = 2048
F = 64
K = 64
BIN0 = 32
W = 2 * F
SUB = 8
TILES = 4
SPAN = SUB * TILES
STEPS = K // SUB
HALF = SUB // 2
MOST = 8
VMEM = pl.BlockSpec(memory_space=pltpu.VMEM)
HBM = pl.BlockSpec(memory_space=pltpu.HBM)


def fill_table(table_ref):
    fine = 64

    def angle(rows, every, turn):
        n = lax.broadcasted_iota(jnp.int32, (rows, W), 0) * every
        lane = lax.broadcasted_iota(jnp.int32, (rows, W), 1)
        phase = n * (BIN0 + lax.rem(lane, F)) + jnp.where(lane < F, 0, S // 4) * (every == 1) + turn
        return jnp.cos(lax.rem(phase, S).astype(jnp.float32) * (2.0 * math.pi / S))

    cos_a, sin_a = angle(S // fine, fine, 0), angle(S // fine, fine, 3 * S // 4)
    cos_b, sin_b = angle(fine, 1, 0), angle(fine, 1, 3 * S // 4)
    for i in range(S // fine):
        rows = cos_a[i : i + 1] * cos_b - sin_a[i : i + 1] * sin_b
        table_ref[fine * i : fine * (i + 1)] = rows.astype(jnp.bfloat16)


def whiten_kernel(jobs, pair, has_table, strain_hbm, *refs):
    refs = list(refs)
    table_ref = refs.pop(0) if has_table else None
    outs = [refs.pop(0) for _ in jobs]
    made_ref = None if has_table else refs.pop(0)
    sems, bufs = refs[0], refs[1:]
    me = lax.axis_index("rec")
    copies = []
    for (start, rows), buf in zip(jobs, bufs):
        at = pl.multiple_of(start(me), rows)
        for r in range(0, buf.shape[0], pair):
            copy = pltpu.make_async_copy(
                strain_hbm.at[pl.ds(r, pair), pl.ds(at, rows), :],
                buf.at[pl.ds(r, pair)],
                sems.at[len(copies)],
            )
            copy.start()
            copies.append(copy)
    if not has_table:
        fill_table(made_ref)
        table_ref = made_ref
    at = 0
    for (_, rows), buf, out in zip(jobs, bufs, outs):
        for r in range(0, buf.shape[0], pair):
            copies[at].wait()
            at += 1
            block = buf[r : r + pair].reshape(pair * rows, S)
            spec = jnp.dot(block, table_ref[...], preferred_element_type=jnp.float32)
            power = jnp.sum(spec * spec, axis=-1, keepdims=True) * (1.0 / F)
            out[r : r + pair] = (spec * lax.rsqrt(power + 1e-06)).reshape(pair, rows, W)


def whiten(strain, jobs, pair, table=None):
    records = strain.shape[0]
    total = sum(rows for _, rows in jobs)
    outs = [jax.ShapeDtypeStruct((records, rows, W), jnp.float32) for _, rows in jobs]
    if table is None:
        outs.append(jax.ShapeDtypeStruct((S, W), jnp.bfloat16))
    return pl.pallas_call(
        functools.partial(whiten_kernel, jobs, pair, table is not None),
        out_shape=outs,
        in_specs=[HBM] + ([] if table is None else [VMEM]),
        out_specs=[VMEM] * len(outs),
        scratch_shapes=[pltpu.SemaphoreType.DMA((len(jobs) * (records // pair),))]
        + [pltpu.VMEM((records, rows, S), jnp.bfloat16) for _, rows in jobs],
        compiler_params=pltpu.CompilerParams(vmem_limit_bytes=50 * 2**20),
        cost_estimate=pl.CostEstimate(
            flops=2 * records * total * S * W,
            bytes_accessed=2 * records * total * S,
            transcendentals=0,
        ),
        name="whiten",
    )(strain, *([] if table is None else [table]))


def halo_kernel(size, own_ref, *refs):
    mains, below_ref, outs = refs[: size - 1], refs[size - 1], refs[size:]
    me = lax.axis_index("rec")
    blocks = [own_ref] + list(mains)
    for by in range(size):
        target = lax.bitwise_xor(me, by)
        out = outs[by]
        at = out.shape[1] - K
        if at:
            out[:, :at] = blocks[by][:, :at]
        for other in range(size):
            if other != by:

                @pl.when((target < size - 1) & (lax.bitwise_xor(me, other) == target + 1))
                def _():
                    out[:, at:] = blocks[other][:, :K]

        @pl.when(target == size - 1)
        def _():
            out[:, at:] = below_ref[...]


def prepare(scale, parts, g, r, a_ref, b_ref):
    low = lax.broadcasted_iota(jnp.int32, (1, W), 1) < F
    rows = a_ref.shape[2]
    at = 0
    for part in parts:
        w = part[r]
        turned = pltpu.roll(w, F, 1)
        b_ref[0, g, at : at + w.shape[0]] = jnp.where(low, turned - w, -(w + turned))
        b_ref[1, g, at : at + w.shape[0]] = jnp.where(low, w, turned)
        if at < rows:
            own, both = turned * scale, (w + turned) * scale
            n = min(rows - at, w.shape[0])
            a_ref[0, g, at : at + n] = own[:n]
            a_ref[1, g, at : at + n] = both[:n]
        at += w.shape[0]


def pack(g, b_ref):
    low = lax.broadcasted_iota(jnp.int32, (1, W), 1) < F
    ext = b_ref.shape[2] - SUB
    here = b_ref[1, g, 0:ext]
    there = b_ref[1, g, HALF : HALF + ext]
    b_ref[1, g, 0:ext] = jnp.where(low, here, there)


def step(q, tiles, row0, records, a_ref, b_ref, acc_ref, out_ref):
    low = lax.broadcasted_iota(jnp.int32, (SUB, W), 1) < F

    def add(total, term):
        return term if total is None else total + term

    for u in range(HALF):
        s = row0 + SUB * q + u
        places, sums = [], []
        for i in tiles:
            rows = pl.ds(pl.multiple_of(row0 + SUB * i, SUB), SUB)
            k = SUB * (q - i) + u
            cols = [pl.ds(pl.multiple_of(n * W, W), W) for n in (k, k + HALF)]
            places.append([(rows, col) for col in cols])
            sums.append([None] + [None if acc_ref is None else acc_ref[at] for at in places[-1]])
        for g in records:
            both = b_ref[1, g, pl.ds(s, SUB)]
            first = b_ref[0, g, pl.ds(s, SUB)]
            second = b_ref[0, g, pl.ds(s + HALF, SUB)]
            for x, i in enumerate(tiles):
                own = a_ref[0, g, pl.ds(row0 + SUB * i, SUB)]
                whole = a_ref[1, g, pl.ds(row0 + SUB * i, SUB)]
                p, t1, t2 = sums[x]
                sums[x] = [add(p, whole * both), add(t1, own * first), add(t2, own * second)]
        for (here, there), (p, t1, t2) in zip(places, sums):
            turned = pltpu.roll(p, F, 1)
            out_ref[here] = t1 + jnp.where(low, p, turned)
            out_ref[there] = t2 + jnp.where(low, turned, p)


def sweep(records, region, rows, a_ref, b_ref, acc_ref, out_ref):
    spans = rows // SPAN
    last = STEPS + TILES - 1
    bound = rows // SUB - 1
    args = (records, a_ref, b_ref, acc_ref, out_ref)

    def run(q, tiles, row0):
        step(q, tiles, row0, *args)

    def span(c, carry):
        row0 = pl.multiple_of(c * SPAN, SPAN)
        edge = bound - TILES * c
        lo, hi = TILES - 1, STEPS
        if region == "main":
            hi = jnp.clip(edge, TILES - 1, STEPS)
        if region == "halo":
            lo = jnp.clip(edge, TILES - 1, STEPS)
        if region != "halo":
            for q in range(TILES - 1):
                run(q, list(range(q + 1)), row0)
        lax.fori_loop(lo, hi, lambda q, n: (run(q, list(range(TILES)), row0), n)[1], 0)

        def tail():
            for q in range(STEPS, last):
                run(q, list(range(q - STEPS + 1, TILES)), row0)

        if region == "main":
            pl.when(edge >= last)(tail)
        else:
            tail()
        return carry

    first = spans - STEPS // TILES if region == "halo" else 0
    lax.fori_loop(first, spans, span, 0)


def cross_kernel(scale, counts, passes, has_acc, rows, *refs):
    refs = list(refs)
    acc_ref = refs.pop(0) if has_acc else None
    groups = [[refs.pop(0) for _ in range(n)] for n in counts]
    out_ref, a_ref, b_ref = refs
    g = 0
    for parts in groups:
        for r in range(parts[0].shape[0]):
            prepare(scale, parts, g, r, a_ref, b_ref)
            pack(g, b_ref)
            g += 1
    for records, region in passes:
        sweep(records, region, rows, a_ref, b_ref, acc_ref, out_ref)


def finish_kernel(scale, records, rows, acc_ref, main_ref, halo_ref, out_hbm, tail_ref, a_ref, b_ref, sems):
    half = rows - K
    top = pltpu.make_async_copy(acc_ref.at[pl.ds(0, half)], out_hbm.at[pl.ds(0, half)], sems.at[0])
    top.start()
    copies = [top]
    tiles = K // SUB

    def slab(i, lo, hi, source, shift):
        return pltpu.make_async_copy(
            source.at[pl.ds(half + SUB * i - shift, SUB), pl.ds(lo * W, (hi - lo) * W)],
            out_hbm.at[pl.ds(half + SUB * i, SUB), pl.ds(lo * W, (hi - lo) * W)],
            sems.at[len(copies)],
        )

    for i in range(tiles - 1):
        copy = slab(i, 0, K - SUB * (i + 1), acc_ref, 0)
        copy.start()
        copies.append(copy)
    for r in range(records):
        prepare(scale, [main_ref, halo_ref], r, r, a_ref, b_ref)
        pack(r, b_ref)
    sweep(range(records), "halo", rows, a_ref, b_ref, acc_ref, tail_ref)
    for i in range(tiles):
        copy = slab(i, K - SUB * (i + 1), K, tail_ref, 0)
        copy.start()
        copies.append(copy)
    for copy in copies:
        copy.wait()


def cost(records, rows):
    return pl.CostEstimate(flops=500 * records * rows * K * W, bytes_accessed=0, transcendentals=0)


def factors(records, rows):
    return [
        pltpu.VMEM((2, records, rows, W), jnp.float32),
        pltpu.VMEM((2, records, rows + K + SUB, W), jnp.float32),
    ]


def cross(groups, passes, rows, scale, acc=None):
    records = sum(g[0].shape[0] for g in groups)
    flat = [p for g in groups for p in g]
    return pl.pallas_call(
        functools.partial(
            cross_kernel, scale, [len(g) for g in groups], passes, acc is not None, rows
        ),
        out_shape=jax.ShapeDtypeStruct((rows, K * W), jnp.float32),
        in_specs=[VMEM] * (len(flat) + (acc is not None)),
        out_specs=VMEM,
        scratch_shapes=factors(records, rows),
        input_output_aliases={0: 0} if acc is not None else {},
        compiler_params=pltpu.CompilerParams(vmem_limit_bytes=28 * 2**20),
        cost_estimate=cost(records, rows),
        name="cross",
    )(*([acc] if acc is not None else []), *flat)


def finish(acc, main, halo, scale):
    records, rows, _ = main.shape
    return pl.pallas_call(
        functools.partial(finish_kernel, scale, records, rows),
        out_shape=jax.ShapeDtypeStruct((rows, K * W), jnp.float32),
        in_specs=[VMEM] * 3,
        out_specs=HBM,
        scratch_shapes=[pltpu.VMEM((rows, K * W), jnp.float32)]
        + factors(records, rows)
        + [pltpu.SemaphoreType.DMA((2 * K // SUB,))],
        compiler_params=pltpu.CompilerParams(vmem_limit_bytes=28 * 2**20),
        cost_estimate=cost(records, rows),
        name="finish",
    )(acc, main, halo)


def send(shard, by):
    size = lax.axis_size("rec")
    return lax.ppermute(shard, "rec", [(i, i ^ by) for i in range(size)])


def shifted(shard, axis, by):
    length = lax.axis_size(axis)
    pairs = [(i, i + by) for i in range(length) if 0 <= i + by < length]
    return lax.ppermute(shard, axis, pairs)


def per_device(strain):
    records, channels, _ = strain.shape
    size = lax.axis_size("rec")
    rows = channels // size
    scale = 1.0 / (records * size)
    if size == 4 and rows == 2 * K and records <= HALF:
        return four(strain, rows, scale)
    return general(strain, rows, scale)


def four(strain, rows, scale):
    records = strain.shape[0]
    pair = 2 if records % 2 == 0 else 1

    def block(by):
        return (lambda me: lax.bitwise_xor(me, by) * rows, rows)

    far, head, table = whiten(strain, [block(3), (lambda me: 0, K)], pair)
    far_in = send(far, 3)
    below = shifted(head, "chan", -1)
    one, two, own = whiten(strain, [block(1), block(2), block(0)], pair, table)
    full = jax.ShapeDtypeStruct((records, rows + K, W), jnp.float32)
    short = jax.ShapeDtypeStruct((records, K, W), jnp.float32)
    own_halo, one, two, far_halo = pl.pallas_call(
        functools.partial(halo_kernel, 4),
        out_shape=[short, full, full, short],
        in_specs=[VMEM] * 5,
        out_specs=[VMEM] * 4,
        compiler_params=pltpu.CompilerParams(vmem_limit_bytes=16 * 2**20),
        name="halo",
    )(own, one, two, far, below)
    one_in = send(one, 1)
    two_in = send(two, 2)
    far_halo_in = send(far_halo, 3)
    near = range(records)
    pairs = range(2 * records)
    acc = cross([[own, own_halo], [far_in]], [(pairs, "main"), (near, "halo")], rows, scale)
    acc = cross([[one_in], [two_in]], [(pairs, "all")], rows, scale, acc)
    return finish(acc, far_in, far_halo_in, scale)


def general(strain, rows, scale):
    records, channels, _ = strain.shape
    size = lax.axis_size("rec")
    me = lax.axis_index("rec")
    spectra, _ = whiten(strain, [(lambda me: 0, channels)], 1)
    below = shifted(spectra[:, :K], "chan", -1)
    extended = jnp.concatenate([spectra, below], axis=1)
    acc = None
    for by in range(size):
        to = lax.rem(me + by, size)
        part = lax.dynamic_slice_in_dim(extended, to * rows, rows + K, 1)
        if by:
            part = lax.ppermute(part, "rec", [(i, (i + by) % size) for i in range(size)])
        for r in range(0, records, MOST):
            some = part[r : r + MOST]
            acc = cross([[some]], [(range(some.shape[0]), "all")], rows, scale, acc)
    return acc


def solution(mesh):
    placed = (P("rec", "chan", None),)
    return jax.shard_map(
        per_device, mesh=mesh, in_specs=placed, out_specs=P(("chan", "rec"), None), check_vma=False
    )
```

time: 304 us -> 36.3 us (0.12)
  waiting for transfers between devices: 161 us -> 8.26 us
  local copies, waits for them, and re-layouts: 89.7 us -> 0 us
  other arithmetic: 24.6 us -> 0 us
  Pallas kernels: 0 us -> 19.1 us
  between operations: 13.6 us -> 0.07 us
  matrix products: 13.2 us -> 0 us
  starting transfers between devices: 1.47 us -> 8.79 us
    reduce_scatter x1 -> x0, waiting for transfers between devices: 160 us -> none  [per_device(): lax.psum_scatter(record_sum(whitened, extended, rows_out * lax.axis_size(...]
    unnamed x127 -> x0, local copies, waits for them, and re-layouts: 83.4 us -> none
    reduce_sum x8 -> x0, other arithmetic: 19.9 us -> none  [record_sum(): cross_im = jnp.sum(a_im * b_re - a_re * b_im, axis=0)]
    pallas_call x0 -> x6, Pallas kernels: none -> 19.1 us  [the longest x2 9.41 us: cross(): pl.pallas_call(functools.partial(cross_kernel, scale, [len(g) for g in gr...]
    dot_general x2 -> x0, matrix products: 13.2 us -> none  [the longest x1 6.66 us: whiten(): spec_im = -jnp.dot(block, sin_table, preferred_element_type=jnp.float32)]
    ppermute x0 -> x4, waiting for transfers between devices: none -> 8.25 us  [send(): return lax.ppermute(shard, 'rec', [(i, i ^ by) for i in range(size)])]
    ppermute x0 -> x4, starting transfers between devices: none -> 7.51 us  [send(): return lax.ppermute(shard, 'rec', [(i, i ^ by) for i in range(size)])]
    div x1 -> x0, local copies, waits for them, and re-layouts: 5.59 us -> none  [per_device(): return summed / records]
  transfers between devices with their start and end apart: 2 -> 5, of which waited for: 2 -> 2; matrix products, arithmetic and copies ran while one was open for 0% -> 0% of each run, Pallas kernels for 0% -> 38%
where the time goes in v2:
time: 36.3 us; the launch traced here: 36.2 us
  Pallas kernels  19.1 us (53%)
  starting transfers between devices  8.79 us (24%)
  waiting for transfers between devices  8.26 us (23%)
    pallas_call x2, Pallas kernels, cross(): pl.pallas_call(functools.partial(cross_kernel, scale, [len(g) for g in gr...  9.41 us
    ppermute x4, waiting for transfers between devices, send(): return lax.ppermute(shard, 'rec', [(i, i ^ by) for i in range(size)])  8.25 us
    ppermute x4, starting transfers between devices, send(): return lax.ppermute(shard, 'rec', [(i, i ^ by) for i in range(size)])  7.51 us
    pallas_call x2, Pallas kernels, whiten(): pl.pallas_call(functools.partial(whiten_kernel, jobs, pair, table is not...  7.38 us
    pallas_call x1, Pallas kernels, finish(): pl.pallas_call(functools.partial(finish_kernel, scale, records, rows), ou...  2.15 us
    ppermute x1, starting transfers between devices, shifted(): return lax.ppermute(shard, axis, pairs)  1.28 us
  transfers between devices with their start and end apart: 5, of which 2 were waited for; matrix products, arithmetic and copies ran while one was open for 0% of the time, Pallas kernels for 38%

profile of v2, /device:TPU:0, one launch (start us, length us, event | category | flops | bytes accessed | tf_op | source)
XLA Modules:
  0.0 36.2 jit_solution(275777824966769168)
XLA Ops:
  0.0 3.0 %whiten.2 = (f32[4,128,128]{2,1,0:T(8,128)S(1)}, f32[4,64,128]{2,1,0:T(8,128)S(1)}, bf16[2048,128]{1,0:T(8,128)(2,1)S(1)}) custom-call(bf16[4,512,2048]{2,1,0:T(8,128)(2,1)} %strain_hbm.3), custom_call_target="tpu_custom_call" | custom-call | flops 402653184 | bytes 3145728 | tf_op jit(solution)/shard_map/whiten/pallas_call | solution.py:80
  3.0 4.0 %collective-permute-start.1 = (f32[4,128,128]{2,1,0:T(8,128)S(1)}, f32[4,128,128]{2,1,0:T(8,128)S(1)}, u32[]{:S(2)}, u32[]{:S(2)}) collective-permute-start(f32[4,128,128]{2,1,0:T(8,128)S(1)} %get-tuple-element.19.refs_2_), channel_id=1, source_target_pairs={{0,3},{1,2},{2,1},{3,0},{4,7},{5,6},{6,5},{7,4},{8,11},{9,10},{10,... | collective-permute-start | bytes 786440 | tf_op jit(solution)/shard_map/ppermute | solution.py:302
  7.0 1.3 %collective-permute-start = (f32[4,64,128]{2,1,0:T(8,128)S(1)}, f32[4,64,128]{2,1,0:T(8,128)S(1)}, u32[]{:S(2)}, u32[]{:S(2)}) collective-permute-start(f32[4,64,128]{2,1,0:T(8,128)S(1)} %get-tuple-element.20), channel_id=1, source_target_pairs={{4,0},{8,4},{12,8},{16,12},{20,16},{24,20},{28,24},{5,1},{9,5},{13... | collective-permute-start | bytes 393224 | tf_op jit(solution)/shard_map/ppermute | solution.py:308
  8.3 4.3 %whiten.3 = (f32[4,128,128]{2,1,0:T(8,128)S(1)}, f32[4,128,128]{2,1,0:T(8,128)S(1)}, f32[4,128,128]{2,1,0:T(8,128)S(1)}) custom-call(bf16[4,512,2048]{2,1,0:T(8,128)(2,1)} %strain_hbm.3, bf16[2048,128]{1,0:T(8,128)(2,1)S(1)} %get-tuple-element.15.refs_0_), custom_call_target="tpu_custom_call" | custom-call | flops 805306368 | bytes 6291456 | tf_op jit(solution)/shard_map/whiten/pallas_call | solution.py:80
  12.6 0.0 collective-permute-done.refs_3_
  12.7 0.1 halo.1
  12.8 0.1 collective-permute-start.4
  12.9 1.9 %collective-permute-start.2 = (f32[4,192,128]{2,1,0:T(8,128)S(1)}, f32[4,192,128]{2,1,0:T(8,128)S(1)}, u32[]{:S(2)}, u32[]{:S(2)}) collective-permute-start(f32[4,192,128]{2,1,0:T(8,128)S(1)} %get-tuple-element.22), channel_id=1, source_target_pairs={{0,1},{1,0},{2,3},{3,2},{4,5},{5,4},{6,7},{7,6},{8,9},{9,8},{10,11... | collective-permute-start | bytes 1179656 | tf_op jit(solution)/shard_map/ppermute | solution.py:302
  14.8 1.5 %collective-permute-start.3 = (f32[4,192,128]{2,1,0:T(8,128)S(1)}, f32[4,192,128]{2,1,0:T(8,128)S(1)}, u32[]{:S(2)}, u32[]{:S(2)}) collective-permute-start(f32[4,192,128]{2,1,0:T(8,128)S(1)} %get-tuple-element.23), channel_id=1, source_target_pairs={{0,2},{1,3},{2,0},{3,1},{4,6},{5,7},{6,4},{7,5},{8,10},{9,11},{10,... | collective-permute-start | bytes 1179656 | tf_op jit(solution)/shard_map/ppermute | solution.py:302
  16.4 0.0 collective-permute-done.1.refs_2_.main_ref
  16.4 3.9 %cross.2.refs_0_ = f32[128,8192]{1,0:T(8,128)S(1)} custom-call(f32[4,128,128]{2,1,0:T(8,128)S(1)} %get-tuple-element.16.own_ref.refs_0_, f32[4,64,128]{2,1,0:T(8,128)S(1)} %get-tuple-element.21.refs_1_, f32[4,128,128]{2,1,0:T(8,128)S(1)} %collective-permute-done.1.refs_2_.main_ref), custom_call_target="tpu_custom_call" | custom-call | flops 4194304000 | tf_op jit(solution)/shard_map/cross/pallas_call | solution.py:269
  20.3 7.1 %collective-permute-done.2.refs_1_ = f32[4,192,128]{2,1,0:T(8,128)S(1)} collective-permute-done((f32[4,192,128]{2,1,0:T(8,128)S(1)}, f32[4,192,128]{2,1,0:T(8,128)S(1)}, u32[]{:S(2)}, u32[]{:S(2)}) %collective-permute-start.2) | collective-permute-done | bytes 393248 | tf_op jit(solution)/shard_map/ppermute | solution.py:302
  27.4 1.1 %collective-permute-done.3.refs_2_ = f32[4,192,128]{2,1,0:T(8,128)S(1)} collective-permute-done((f32[4,192,128]{2,1,0:T(8,128)S(1)}, f32[4,192,128]{2,1,0:T(8,128)S(1)}, u32[]{:S(2)}, u32[]{:S(2)}) %collective-permute-start.3) | collective-permute-done | bytes 393248 | tf_op jit(solution)/shard_map/ppermute | solution.py:302
  28.6 5.5 %cross.3.acc_ref = f32[128,8192]{1,0:T(8,128)S(1)} custom-call(f32[128,8192]{1,0:T(8,128)S(1)} %cross.2.refs_0_, f32[4,192,128]{2,1,0:T(8,128)S(1)} %collective-permute-done.2.refs_1_, f32[4,192,128]{2,1,0:T(8,128)S(1)} %collective-permute-done.3.refs_2_), custom_call_target="tpu_custom_call", output_to_operand_aliasing={{}: (0, {})} | custom-call | flops 4194304000 | tf_op jit(solution)/shard_map/cross/pallas_call | solution.py:269
  34.0 0.0 collective-permute-done.4.halo_ref
  34.0 2.1 %finish.1 = f32[128,8192]{1,0:T(8,128)} custom-call(f32[128,8192]{1,0:T(8,128)S(1)} %cross.3.acc_ref, f32[4,128,128]{2,1,0:T(8,128)S(1)} %collective-permute-done.1.refs_2_.main_ref, f32[4,64,128]{2,1,0:T(8,128)S(1)} %collective-permute-done.4.halo_ref), custom_call_target="tpu_custom_call" | custom-call | flops 2097152000 | tf_op jit(solution)/shard_map/finish/pallas_call | solution.py:286
Async XLA Ops:
  3.0 13.3 %collective-permute-start.1 = (f32[4,128,128]{2,1,0:T(8,128)S(1)}, f32[4,128,128]{2,1,0:T(8,128)S(1)}, u32[]{:S(2)}, u32[]{:S(2)}) collective-permute-start(f32[4,128,128]{2,1,0:T(8,128)S(1)} %get-tuple-element.19.refs_2_), channel_id=1, source_target_pairs={{0,3},{1,2},{2,1},{3,0},{4,7},{5,6},{6,5},{7,4},{8,11},{9,10},{10,... | collective-permute-start | bytes 786440 | tf_op jit(solution)/shard_map/ppermute | solution.py:302
  7.0 5.6 %collective-permute-start = (f32[4,64,128]{2,1,0:T(8,128)S(1)}, f32[4,64,128]{2,1,0:T(8,128)S(1)}, u32[]{:S(2)}, u32[]{:S(2)}) collective-permute-start(f32[4,64,128]{2,1,0:T(8,128)S(1)} %get-tuple-element.20), channel_id=1, source_target_pairs={{4,0},{8,4},{12,8},{16,12},{20,16},{24,20},{28,24},{5,1},{9,5},{13... | collective-permute-start | bytes 393224 | tf_op jit(solution)/shard_map/ppermute | solution.py:308
  12.8 21.2 %collective-permute-start.4 = (f32[4,64,128]{2,1,0:T(8,128)S(1)}, f32[4,64,128]{2,1,0:T(8,128)S(1)}, u32[]{:S(2)}, u32[]{:S(2)}) collective-permute-start(f32[4,64,128]{2,1,0:T(8,128)S(1)} %get-tuple-element.24), channel_id=1, source_target_pairs={{0,3},{1,2},{2,1},{3,0},{4,7},{5,6},{6,5},{7,4},{8,11},{9,10},{10,... | collective-permute-start | bytes 393224 | tf_op jit(solution)/shard_map/ppermute | solution.py:302
  12.9 14.6 %collective-permute-start.2 = (f32[4,192,128]{2,1,0:T(8,128)S(1)}, f32[4,192,128]{2,1,0:T(8,128)S(1)}, u32[]{:S(2)}, u32[]{:S(2)}) collective-permute-start(f32[4,192,128]{2,1,0:T(8,128)S(1)} %get-tuple-element.22), channel_id=1, source_target_pairs={{0,1},{1,0},{2,3},{3,2},{4,5},{5,4},{6,7},{7,6},{8,9},{9,8},{10,11... | collective-permute-start | bytes 1179656 | tf_op jit(solution)/shard_map/ppermute | solution.py:302
  14.8 13.7 %collective-permute-start.3 = (f32[4,192,128]{2,1,0:T(8,128)S(1)}, f32[4,192,128]{2,1,0:T(8,128)S(1)}, u32[]{:S(2)}, u32[]{:S(2)}) collective-permute-start(f32[4,192,128]{2,1,0:T(8,128)S(1)} %get-tuple-element.23), channel_id=1, source_target_pairs={{0,2},{1,3},{2,0},{3,1},{4,6},{5,7},{6,4},{7,5},{8,10},{9,11},{10,... | collective-permute-start | bytes 1179656 | tf_op jit(solution)/shard_map/ppermute | solution.py:302

commit v3 on v2

v3 whole, which is shorter than its diff:
```python
import functools
import math

import jax
import jax.numpy as jnp
from jax import lax
from jax.experimental import pallas as pl
from jax.experimental.pallas import tpu as pltpu
from jax.sharding import PartitionSpec as P

S = 2048
F = 64
K = 64
BIN0 = 32
W = 2 * F
SUB = 8
STEPS = K // SUB
HALF = SUB // 2
MOST = 8
VMEM = pl.BlockSpec(memory_space=pltpu.VMEM)
HBM = pl.BlockSpec(memory_space=pltpu.HBM)


def fill_table(table_ref):
    fine = 64

    def angle(rows, every, turn):
        n = lax.broadcasted_iota(jnp.int32, (rows, W), 0) * every
        lane = lax.broadcasted_iota(jnp.int32, (rows, W), 1)
        phase = n * (BIN0 + lax.rem(lane, F)) + jnp.where(lane < F, 0, S // 4) * (every == 1) + turn
        return jnp.cos(lax.rem(phase, S).astype(jnp.float32) * (2.0 * math.pi / S))

    cos_a, sin_a = angle(S // fine, fine, 0), angle(S // fine, fine, 3 * S // 4)
    cos_b, sin_b = angle(fine, 1, 0), angle(fine, 1, 3 * S // 4)
    for i in range(S // fine):
        rows = cos_a[i : i + 1] * cos_b - sin_a[i : i + 1] * sin_b
        table_ref[fine * i : fine * (i + 1)] = rows.astype(jnp.bfloat16)


def whiten_kernel(jobs, pair, strain_hbm, *refs):
    outs, head_ref, refs = refs[: len(jobs)], refs[len(jobs)], refs[len(jobs) + 1 :]
    table_ref, sems, bufs = refs[0], refs[1], refs[2:]
    me = lax.axis_index("rec")
    copies = []
    for (start, rows), buf in zip(jobs, bufs):
        at = pl.multiple_of(start(me), rows)
        for r in range(0, buf.shape[0], pair):
            copy = pltpu.make_async_copy(
                strain_hbm.at[pl.ds(r, pair), pl.ds(at, rows), :],
                buf.at[pl.ds(r, pair)],
                sems.at[len(copies)],
            )
            copy.start()
            copies.append(copy)
    fill_table(table_ref)
    at = 0
    for (start, rows), buf, out in zip(jobs, bufs, outs):
        for r in range(0, buf.shape[0], pair):
            copies[at].wait()
            at += 1
            block = buf[r : r + pair].reshape(pair * rows, S)
            spec = jnp.dot(block, table_ref[...], preferred_element_type=jnp.float32)
            power = jnp.sum(spec * spec, axis=-1, keepdims=True) * (1.0 / F)
            out[r : r + pair] = (spec * lax.rsqrt(power + 1e-06)).reshape(pair, rows, W)

        @pl.when(start(me) == 0)
        def _():
            head_ref[...] = out[:, :K]


def whiten(strain, jobs, pair):
    records = strain.shape[0]
    total = sum(rows for _, rows in jobs)
    outs = [jax.ShapeDtypeStruct((records, rows, W), jnp.float32) for _, rows in jobs]
    outs.append(jax.ShapeDtypeStruct((records, K, W), jnp.float32))
    return pl.pallas_call(
        functools.partial(whiten_kernel, jobs, pair),
        out_shape=outs,
        in_specs=[HBM],
        out_specs=[VMEM] * len(outs),
        scratch_shapes=[
            pltpu.VMEM((S, W), jnp.bfloat16),
            pltpu.SemaphoreType.DMA((len(jobs) * (records // pair),)),
        ]
        + [pltpu.VMEM((records, rows, S), jnp.bfloat16) for _, rows in jobs],
        compiler_params=pltpu.CompilerParams(vmem_limit_bytes=50 * 2**20),
        cost_estimate=pl.CostEstimate(
            flops=2 * records * total * S * W,
            bytes_accessed=2 * records * total * S,
            transcendentals=0,
        ),
        name="whiten",
    )(strain)


def halo_kernel(size, *refs):
    blocks, below_ref, outs = refs[:size], refs[size], refs[size + 1 :]
    me = lax.axis_index("rec")
    for by, out in enumerate(outs):
        target = lax.bitwise_xor(me, by)
        for other in range(size):
            if other != by:

                @pl.when((target < size - 1) & (lax.bitwise_xor(me, other) == target + 1))
                def _():
                    out[...] = blocks[other][:, :K]

        @pl.when(target == size - 1)
        def _():
            out[...] = below_ref[...]


def halos(blocks, below):
    size = len(blocks)
    return pl.pallas_call(
        functools.partial(halo_kernel, size),
        out_shape=[jax.ShapeDtypeStruct(below.shape, jnp.float32)] * size,
        in_specs=[VMEM] * (size + 1),
        out_specs=[VMEM] * size,
        compiler_params=pltpu.CompilerParams(vmem_limit_bytes=16 * 2**20),
        name="halo",
    )(*blocks, below)


def low_half(rows=1):
    return lax.broadcasted_iota(jnp.int32, (rows, W), 1) < F


def prepare(scale, parts, r, g, a_ref, b_ref, own_from=0, partner_from=0):
    low = low_half()
    rows = a_ref.shape[2]
    w = parts[0][r, own_from:rows]
    turned = pltpu.roll(w, F, 1)
    a_ref[0, g, own_from:rows] = turned * scale
    a_ref[1, g, own_from:rows] = (w + turned) * scale
    at = 0
    for part in parts:
        n = part.shape[1]
        skip = max(partner_from - at, 0)
        w = part[r, skip:]
        turned = pltpu.roll(w, F, 1)
        b_ref[0, g, at + skip : at + n] = jnp.where(low, turned - w, -(w + turned))
        b_ref[1, g, at + skip : at + n] = jnp.where(low, w, turned)
        at += n
    here = b_ref[1, g, partner_from:at]
    there = b_ref[1, g, partner_from + HALF : at + HALF]
    b_ref[1, g, partner_from:at] = jnp.where(low, here, there)


def step(q, tiles, row0, records, a_ref, b_ref, acc_ref, out_ref):
    low = low_half(SUB)

    def add(total, term):
        return term if total is None else total + term

    for u in range(HALF):
        s = row0 + SUB * q + u
        places, sums = [], []
        for i in tiles:
            rows = pl.ds(pl.multiple_of(row0 + SUB * i, SUB), SUB)
            k = SUB * (q - i) + u
            cols = [pl.ds(pl.multiple_of(n * W, W), W) for n in (k, k + HALF)]
            places.append([(rows, col) for col in cols])
            sums.append([None] + [None if acc_ref is None else acc_ref[at] for at in places[-1]])
        for g in records:
            both = b_ref[1, g, pl.ds(s, SUB)]
            first = b_ref[0, g, pl.ds(s, SUB)]
            second = b_ref[0, g, pl.ds(s + HALF, SUB)]
            for x, i in enumerate(tiles):
                own = a_ref[0, g, pl.ds(pl.multiple_of(row0 + SUB * i, SUB), SUB)]
                whole = a_ref[1, g, pl.ds(pl.multiple_of(row0 + SUB * i, SUB), SUB)]
                p, t1, t2 = sums[x]
                sums[x] = [add(p, whole * both), add(t1, own * first), add(t2, own * second)]
        for (here, there), (p, t1, t2) in zip(places, sums):
            turned = pltpu.roll(p, F, 1)
            out_ref[here] = t1 + jnp.where(low, p, turned)
            out_ref[there] = t2 + jnp.where(low, turned, p)


def sweep(records, region, rows, a_ref, b_ref, acc_ref, out_ref):
    tiles = 8 if rows % (8 * SUB) == 0 else 4
    spans = rows // (SUB * tiles)
    last = STEPS + tiles - 1
    bound = rows // SUB - 1
    args = (records, a_ref, b_ref, acc_ref, out_ref)

    def run(q, some, row0):
        step(q, some, row0, *args)

    def span(c, carry):
        row0 = pl.multiple_of(c * (SUB * tiles), SUB * tiles)
        edge = bound - tiles * c
        lo, hi = tiles - 1, STEPS
        if region == "main":
            hi = jnp.clip(edge, tiles - 1, STEPS)
        if region == "halo":
            lo = jnp.clip(edge, tiles - 1, STEPS)
        if region != "halo":
            for q in range(tiles - 1):
                run(q, list(range(q + 1)), row0)
        lax.fori_loop(lo, hi, lambda q, n: (run(q, list(range(tiles)), row0), n)[1], 0)

        def tail():
            for q in range(STEPS, last):
                run(q, list(range(q - STEPS + 1, tiles)), row0)

        if region == "main":
            pl.when(edge >= last)(tail)
        else:
            tail()
        return carry

    first = spans - STEPS // tiles if region == "halo" else 0
    lax.fori_loop(first, spans, span, 0)


def cross_kernel(scale, counts, region, has_acc, rows, *refs):
    refs = list(refs)
    acc_ref = refs.pop(0) if has_acc else None
    groups = [[refs.pop(0) for _ in range(n)] for n in counts]
    out_ref, a_ref, b_ref = refs
    g = 0
    for parts in groups:
        for r in range(parts[0].shape[0]):
            prepare(scale, parts, r, g, a_ref, b_ref)
            g += 1
    sweep(range(g), region, rows, a_ref, b_ref, acc_ref, out_ref)


def slabs(rows, halo, source, out_hbm, sems):
    top = rows - K
    tiles = K // SUB
    places = [] if halo else [((0, top), (0, K))]
    for i in range(tiles):
        edge = K - SUB * (i + 1)
        lo, hi = (edge, K) if halo else (0, edge)
        if hi > lo:
            places.append(((top + SUB * i, SUB), (lo, hi - lo)))
    copies = []
    for (row, n), (col, m) in places:
        at = (pl.ds(row, n), pl.ds(col * W, m * W))
        copies.append(pltpu.make_async_copy(source.at[at], out_hbm.at[at], sems.at[len(copies)]))
    return copies


def halo_sums(scale, groups, a_ref, b_ref, acc_ref, out_ref):
    rows = a_ref.shape[2]
    g = 0
    for parts in groups:
        for r in range(parts[0].shape[0]):
            prepare(scale, parts, r, g, a_ref, b_ref, rows - K, rows - 2 * SUB)
            g += 1
    sweep(range(g), "halo", rows, a_ref, b_ref, acc_ref, out_ref)


def edge_kernel(scale, count, rows, acc_ref, *refs):
    groups = [refs[2 * i : 2 * i + 2] for i in range(count)]
    out_hbm, tail_ref, a_ref, b_ref, sems = refs[2 * count :]
    copies = slabs(rows, False, acc_ref, out_hbm, sems)
    for copy in copies:
        copy.start()
    halo_sums(scale, groups, a_ref, b_ref, None, tail_ref)
    for copy in copies:
        copy.wait()


def finish_kernel(scale, rows, part_hbm, tail_ref, main_ref, halo_ref, out_hbm, sum_ref, a_ref, b_ref, sems):
    halo_sums(scale, [[main_ref, halo_ref]], a_ref, b_ref, tail_ref, sum_ref)
    copies = slabs(rows, True, sum_ref, out_hbm, sems)
    for copy in copies:
        copy.start()
    for copy in copies:
        copy.wait()


def cost(records, rows):
    return pl.CostEstimate(flops=500 * records * rows * K * W, bytes_accessed=0, transcendentals=0)


def factors(records, rows):
    return [
        pltpu.VMEM((2, records, rows, W), jnp.float32),
        pltpu.VMEM((2, records, rows + K + SUB, W), jnp.float32),
    ]


PARAMS = pltpu.CompilerParams(vmem_limit_bytes=24 * 2**20)


def cross(groups, region, rows, scale, acc=None):
    records = sum(g[0].shape[0] for g in groups)
    flat = [p for g in groups for p in g]
    return pl.pallas_call(
        functools.partial(
            cross_kernel, scale, [len(g) for g in groups], region, acc is not None, rows
        ),
        out_shape=jax.ShapeDtypeStruct((rows, K * W), jnp.float32),
        in_specs=[VMEM] * (len(flat) + (acc is not None)),
        out_specs=VMEM,
        scratch_shapes=factors(records, rows),
        input_output_aliases={0: 0} if acc is not None else {},
        compiler_params=PARAMS,
        cost_estimate=cost(records, rows),
        name="cross",
    )(*([acc] if acc is not None else []), *flat)


def edge(acc, groups, rows, scale):
    records = sum(g[0].shape[0] for g in groups)
    flat = [p for g in groups for p in g]
    out = jax.ShapeDtypeStruct((rows, K * W), jnp.float32)
    return pl.pallas_call(
        functools.partial(edge_kernel, scale, len(groups), rows),
        out_shape=[out, out],
        in_specs=[VMEM] * (1 + len(flat)),
        out_specs=[HBM, VMEM],
        scratch_shapes=factors(records, rows) + [pltpu.SemaphoreType.DMA((K // SUB,))],
        compiler_params=PARAMS,
        cost_estimate=cost(records // 3, rows),
        name="edge",
    )(acc, *flat)


def finish(part, tail, main, halo, scale):
    records, rows, _ = main.shape
    return pl.pallas_call(
        functools.partial(finish_kernel, scale, rows),
        out_shape=jax.ShapeDtypeStruct((rows, K * W), jnp.float32),
        in_specs=[HBM] + [VMEM] * 3,
        out_specs=HBM,
        scratch_shapes=[pltpu.VMEM((rows, K * W), jnp.float32)]
        + factors(records, rows)
        + [pltpu.SemaphoreType.DMA((K // SUB,))],
        input_output_aliases={0: 0},
        compiler_params=PARAMS,
        cost_estimate=cost(records // 3, rows),
        name="finish",
    )(part, tail, main, halo)


def send(shard, by):
    size = lax.axis_size("rec")
    return lax.ppermute(shard, "rec", [(i, i ^ by) for i in range(size)])


def shifted(shard, axis, by):
    length = lax.axis_size(axis)
    pairs = [(i, i + by) for i in range(length) if 0 <= i + by < length]
    return lax.ppermute(shard, axis, pairs)


def per_device(strain):
    records, channels, _ = strain.shape
    size = lax.axis_size("rec")
    rows = channels // size
    scale = 1.0 / (records * size)
    if size == 4 and rows == 2 * K and records <= HALF:
        return four(strain, rows, scale)
    return general(strain, rows, scale)


def four(strain, rows, scale):
    pair = 2 if strain.shape[0] % 2 == 0 else 1

    def block(by):
        return (lambda me: lax.bitwise_xor(me, by) * rows, rows)

    far, one, two, own, head = whiten(strain, [block(3), block(1), block(2), block(0)], pair)
    below = shifted(head, "chan", -1)
    far_in, one_in, two_in = send(far, 3), send(one, 1), send(two, 2)
    own_halo, one_halo, two_halo, far_halo = halos([own, one, two, far], below)
    one_halo_in, two_halo_in, far_halo_in = send(one_halo, 1), send(two_halo, 2), send(far_halo, 3)
    acc = cross([[own], [far_in]], "main", rows, scale)
    acc = cross([[one_in], [two_in]], "main", rows, scale, acc)
    part, tail = edge(
        acc, [[own, own_halo], [one_in, one_halo_in], [two_in, two_halo_in]], rows, scale
    )
    return finish(part, tail, far_in, far_halo_in, scale)


def general(strain, rows, scale):
    records, channels, _ = strain.shape
    size = lax.axis_size("rec")
    me = lax.axis_index("rec")
    spectra, head = whiten(strain, [(lambda me: 0 * me, channels)], 1)
    below = shifted(head, "chan", -1)
    extended = jnp.concatenate([spectra, below], axis=1)
    acc = None
    for by in range(size):
        to = lax.rem(me + by, size)
        part = lax.dynamic_slice_in_dim(extended, to * rows, rows + K, 1)
        if by:
            part = lax.ppermute(part, "rec", [(i, (i + by) % size) for i in range(size)])
        for r in range(0, records, MOST):
            acc = cross([[part[r : r + MOST]]], "all", rows, scale, acc)
    return acc


def solution(mesh):
    placed = (P("rec", "chan", None),)
    return jax.shard_map(
        per_device, mesh=mesh, in_specs=placed, out_specs=P(("chan", "rec"), None), check_vma=False
    )
```

time: 36.3 us -> 30.8 us (0.85)
  waiting for transfers between devices: 8.26 us -> 2.98 us
  Pallas kernels: 19.1 us -> 16.4 us
  starting transfers between devices: 8.79 us -> 11.1 us
    ppermute x4 -> x6, waiting for transfers between devices: 8.25 us -> 1.69 us  [send(): return lax.ppermute(shard, 'rec', [(i, i ^ by) for i in range(size)])]
    pallas_call x2, Pallas kernels: 9.41 us -> 6.32 us  [cross(): pl.pallas_call(functools.partial(cross_kernel, scale, [len(g) for g in gr...]
    ppermute x4 -> x6, starting transfers between devices: 7.51 us -> 9.8 us  [send(): return lax.ppermute(shard, 'rec', [(i, i ^ by) for i in range(size)])]
    ppermute x1, waiting for transfers between devices: 0.01 us -> 1.29 us  [shifted(): return lax.ppermute(shard, axis, pairs)]
    pallas_call x4, Pallas kernels: 9.66 us -> 10.1 us  [the longest x1 5.38 us: whiten(): pl.pallas_call(functools.partial(whiten_kernel, jobs, pair), out_shape=ou...]
  transfers between devices with their start and end apart: 5 -> 7, of which waited for: 2 -> 3; matrix products, arithmetic and copies ran while one was open for 0% -> 0% of each run, Pallas kernels for 38% -> 29%
where the time goes in v3:
time: 30.8 us; the launch traced here: 30.7 us
  Pallas kernels  16.4 us (53%)
  starting transfers between devices  11.1 us (36%)
  waiting for transfers between devices  2.98 us (10%)
    ppermute x6, starting transfers between devices, send(): return lax.ppermute(shard, 'rec', [(i, i ^ by) for i in range(size)])  9.8 us
    pallas_call x2, Pallas kernels, cross(): pl.pallas_call(functools.partial(cross_kernel, scale, [len(g) for g in gr...  6.32 us
    pallas_call x1, Pallas kernels, whiten(): pl.pallas_call(functools.partial(whiten_kernel, jobs, pair), out_shape=ou...  5.38 us
    pallas_call x1, Pallas kernels, edge(): pl.pallas_call(functools.partial(edge_kernel, scale, len(groups), rows),...  2.43 us
    pallas_call x1, Pallas kernels, finish(): pl.pallas_call(functools.partial(finish_kernel, scale, rows), out_shape=j...  1.98 us
    ppermute x6, waiting for transfers between devices, send(): return lax.ppermute(shard, 'rec', [(i, i ^ by) for i in range(size)])  1.69 us
    ppermute x1, waiting for transfers between devices, shifted(): return lax.ppermute(shard, axis, pairs)  1.29 us
    ppermute x1, starting transfers between devices, shifted(): return lax.ppermute(shard, axis, pairs)  1.28 us
  transfers between devices with their start and end apart: 7, of which 3 were waited for; matrix products, arithmetic and copies ran while one was open for 0% of the time, Pallas kernels for 29%

profile of v3, /device:TPU:0, one launch (start us, length us, event | category | flops | bytes accessed | tf_op | source)
XLA Modules:
  0.0 30.7 jit_solution(12009166127463628908)
XLA Ops:
  0.0 5.4 %whiten.1 = (f32[4,128,128]{2,1,0:T(8,128)S(1)}, f32[4,128,128]{2,1,0:T(8,128)S(1)}, f32[4,128,128]{2,1,0:T(8,128)S(1)}, f32[4,128,128]{2,1,0:T(8,128)S(1)}, f32[4,64,128]{2,1,0:T(8,128)S(1)}) custom-call(bf16[4,512,2048]{2,1,0:T(8,128)(2,1)} %strain_hbm.1), custom_call_target="tpu_custom_call" | custom-call | flops 1073741824 | bytes 8388608 | tf_op jit(solution)/shard_map/whiten/pallas_call | solution.py:76
  5.4 4.0 %collective-permute-start = (f32[4,128,128]{2,1,0:T(8,128)S(1)}, f32[4,128,128]{2,1,0:T(8,128)S(1)}, u32[]{:S(2)}, u32[]{:S(2)}) collective-permute-start(f32[4,128,128]{2,1,0:T(8,128)S(1)} %get-tuple-element.17.refs_3_), channel_id=1, source_target_pairs={{0,3},{1,2},{2,1},{3,0},{4,7},{5,6},{6,5},{7,4},{8,11},{9,10},{10,... | collective-permute-start | bytes 786440 | tf_op jit(solution)/shard_map/ppermute | solution.py:343
  9.3 1.3 %collective-permute-start.3 = (f32[4,64,128]{2,1,0:T(8,128)S(1)}, f32[4,64,128]{2,1,0:T(8,128)S(1)}, u32[]{:S(2)}, u32[]{:S(2)}) collective-permute-start(f32[4,64,128]{2,1,0:T(8,128)S(1)} %get-tuple-element.20), channel_id=1, source_target_pairs={{4,0},{8,4},{12,8},{16,12},{20,16},{24,20},{28,24},{5,1},{9,5},{13... | collective-permute-start | bytes 393224 | tf_op jit(solution)/shard_map/ppermute | solution.py:349
  10.6 0.6 %collective-permute-start.1 = (f32[4,128,128]{2,1,0:T(8,128)S(1)}, f32[4,128,128]{2,1,0:T(8,128)S(1)}, u32[]{:S(2)}, u32[]{:S(2)}) collective-permute-start(f32[4,128,128]{2,1,0:T(8,128)S(1)} %get-tuple-element.18.refs_1_), channel_id=1, source_target_pairs={{0,1},{1,0},{2,3},{3,2},{4,5},{5,4},{6,7},{7,6},{8,9},{9,8},{10,11... | collective-permute-start | bytes 786440 | tf_op jit(solution)/shard_map/ppermute | solution.py:343
  11.2 0.1 collective-permute-start.2
  11.3 1.3 %collective-permute-done.3.refs_4_ = f32[4,64,128]{2,1,0:T(8,128)S(1)} collective-permute-done((f32[4,64,128]{2,1,0:T(8,128)S(1)}, f32[4,64,128]{2,1,0:T(8,128)S(1)}, u32[]{:S(2)}, u32[]{:S(2)}) %collective-permute-start.3) | collective-permute-done | bytes 131104 | tf_op jit(solution)/shard_map/ppermute | solution.py:349
  12.6 0.3 halo.1
  12.9 0.7 %collective-permute-start.4 = (f32[4,64,128]{2,1,0:T(8,128)S(1)}, f32[4,64,128]{2,1,0:T(8,128)S(1)}, u32[]{:S(2)}, u32[]{:S(2)}) collective-permute-start(f32[4,64,128]{2,1,0:T(8,128)S(1)} %get-tuple-element.22), channel_id=1, source_target_pairs={{0,1},{1,0},{2,3},{3,2},{4,5},{5,4},{6,7},{7,6},{8,9},{9,8},{10,11... | collective-permute-start | bytes 393224 | tf_op jit(solution)/shard_map/ppermute | solution.py:343
  13.6 1.5 %collective-permute-start.5 = (f32[4,64,128]{2,1,0:T(8,128)S(1)}, f32[4,64,128]{2,1,0:T(8,128)S(1)}, u32[]{:S(2)}, u32[]{:S(2)}) collective-permute-start(f32[4,64,128]{2,1,0:T(8,128)S(1)} %get-tuple-element.23), channel_id=1, source_target_pairs={{0,2},{1,3},{2,0},{3,1},{4,6},{5,7},{6,4},{7,5},{8,10},{9,11},{10,... | collective-permute-start | bytes 393224 | tf_op jit(solution)/shard_map/ppermute | solution.py:343
  15.1 1.4 %collective-permute-done.refs_1_.main_ref = f32[4,128,128]{2,1,0:T(8,128)S(1)} collective-permute-done((f32[4,128,128]{2,1,0:T(8,128)S(1)}, f32[4,128,128]{2,1,0:T(8,128)S(1)}, u32[]{:S(2)}, u32[]{:S(2)}) %collective-permute-start) | collective-permute-done | bytes 262176 | tf_op jit(solution)/shard_map/ppermute | solution.py:343
  16.5 3.0 %collective-permute-start.6 = (f32[4,64,128]{2,1,0:T(8,128)S(1)}, f32[4,64,128]{2,1,0:T(8,128)S(1)}, u32[]{:S(2)}, u32[]{:S(2)}) collective-permute-start(f32[4,64,128]{2,1,0:T(8,128)S(1)} %get-tuple-element.26), channel_id=1, source_target_pairs={{0,3},{1,2},{2,1},{3,0},{4,7},{5,6},{6,5},{7,4},{8,11},{9,10},{10,... | collective-permute-start | bytes 393224 | tf_op jit(solution)/shard_map/ppermute | solution.py:343
  19.4 2.9 %cross.2.refs_0_ = f32[128,8192]{1,0:T(8,128)S(1)} custom-call(f32[4,128,128]{2,1,0:T(8,128)S(1)} %get-tuple-element.16.refs_0_, f32[4,128,128]{2,1,0:T(8,128)S(1)} %collective-permute-done.refs_1_.main_ref), custom_call_target="tpu_custom_call" | custom-call | flops 4194304000 | tf_op jit(solution)/shard_map/cross/pallas_call | solution.py:293
  22.4 0.3 collective-permute-done.1.refs_1_.refs_2_
  22.7 0.0 collective-permute-done.2.refs_2_.refs_4_
  22.7 3.4 %cross.3.acc_ref = f32[128,8192]{1,0:T(8,128)S(1)} custom-call(f32[128,8192]{1,0:T(8,128)S(1)} %cross.2.refs_0_, f32[4,128,128]{2,1,0:T(8,128)S(1)} %collective-permute-done.1.refs_1_.refs_2_, f32[4,128,128]{2,1,0:T(8,128)S(1)} %collective-permute-done.2.refs_2_.refs_4_), custom_call_target="tpu_custom_call", output_to_operand_aliasing={{}: (0, {})} | custom-call | flops 4194304000 | tf_op jit(solution)/shard_map/cross/pallas_call | solution.py:293
  26.1 0.0 collective-permute-done.4.refs_3_
  26.1 0.0 collective-permute-done.5.refs_5_
  26.1 2.4 %edge.1 = (f32[128,8192]{1,0:T(8,128)}, f32[128,8192]{1,0:T(8,128)S(1)}) custom-call(f32[128,8192]{1,0:T(8,128)S(1)} %cross.3.acc_ref, f32[4,128,128]{2,1,0:T(8,128)S(1)} %get-tuple-element.16.refs_0_, f32[4,64,128]{2,1,0:T(8,128)S(1)} %get-tuple-element.21.refs_1_, f32[4,128,128]{2,1,0:T(8,128)S(1)} %collective-permute-done.1.refs_1_.refs_2_, ...), custom_call_target="tpu_custom_call" | custom-call | flops 2097152000 | tf_op jit(solution)/shard_map/edge/pallas_call | solution.py:312
  28.5 0.0 collective-permute-done.6.halo_ref
  28.5 2.0 %finish.1 = f32[128,8192]{1,0:T(8,128)} custom-call(f32[128,8192]{1,0:T(8,128)} %get-tuple-element.24.part_hbm, f32[128,8192]{1,0:T(8,128)S(1)} %get-tuple-element.25.tail_ref, f32[4,128,128]{2,1,0:T(8,128)S(1)} %collective-permute-done.refs_1_.main_ref, f32[4,64,128]{2,1,0:T(8,128)S(1)} %collective-permute-done.6.halo_ref), custom_call_target="tpu_custom_call", output_to_operand_aliasing={{}: (0, {})} | custom-call | flops 524288000 | tf_op jit(solution)/shard_map/finish/pallas_call | solution.py:326
Async XLA Ops:
  5.4 11.1 %collective-permute-start = (f32[4,128,128]{2,1,0:T(8,128)S(1)}, f32[4,128,128]{2,1,0:T(8,128)S(1)}, u32[]{:S(2)}, u32[]{:S(2)}) collective-permute-start(f32[4,128,128]{2,1,0:T(8,128)S(1)} %get-tuple-element.17.refs_3_), channel_id=1, source_target_pairs={{0,3},{1,2},{2,1},{3,0},{4,7},{5,6},{6,5},{7,4},{8,11},{9,10},{10,... | collective-permute-start | bytes 786440 | tf_op jit(solution)/shard_map/ppermute | solution.py:343
  9.3 3.2 %collective-permute-start.3 = (f32[4,64,128]{2,1,0:T(8,128)S(1)}, f32[4,64,128]{2,1,0:T(8,128)S(1)}, u32[]{:S(2)}, u32[]{:S(2)}) collective-permute-start(f32[4,64,128]{2,1,0:T(8,128)S(1)} %get-tuple-element.20), channel_id=1, source_target_pairs={{4,0},{8,4},{12,8},{16,12},{20,16},{24,20},{28,24},{5,1},{9,5},{13... | collective-permute-start | bytes 393224 | tf_op jit(solution)/shard_map/ppermute | solution.py:349
  10.6 12.0 %collective-permute-start.1 = (f32[4,128,128]{2,1,0:T(8,128)S(1)}, f32[4,128,128]{2,1,0:T(8,128)S(1)}, u32[]{:S(2)}, u32[]{:S(2)}) collective-permute-start(f32[4,128,128]{2,1,0:T(8,128)S(1)} %get-tuple-element.18.refs_1_), channel_id=1, source_target_pairs={{0,1},{1,0},{2,3},{3,2},{4,5},{5,4},{6,7},{7,6},{8,9},{9,8},{10,11... | collective-permute-start | bytes 786440 | tf_op jit(solution)/shard_map/ppermute | solution.py:343
  11.2 11.4 %collective-permute-start.2 = (f32[4,128,128]{2,1,0:T(8,128)S(1)}, f32[4,128,128]{2,1,0:T(8,128)S(1)}, u32[]{:S(2)}, u32[]{:S(2)}) collective-permute-start(f32[4,128,128]{2,1,0:T(8,128)S(1)} %get-tuple-element.19.refs_2_), channel_id=1, source_target_pairs={{0,2},{1,3},{2,0},{3,1},{4,6},{5,7},{6,4},{7,5},{8,10},{9,11},{10,... | collective-permute-start | bytes 786440 | tf_op jit(solution)/shard_map/ppermute | solution.py:343
  12.9 13.2 %collective-permute-start.4 = (f32[4,64,128]{2,1,0:T(8,128)S(1)}, f32[4,64,128]{2,1,0:T(8,128)S(1)}, u32[]{:S(2)}, u32[]{:S(2)}) collective-permute-start(f32[4,64,128]{2,1,0:T(8,128)S(1)} %get-tuple-element.22), channel_id=1, source_target_pairs={{0,1},{1,0},{2,3},{3,2},{4,5},{5,4},{6,7},{7,6},{8,9},{9,8},{10,11... | collective-permute-start | bytes 393224 | tf_op jit(solution)/shard_map/ppermute | solution.py:343
  13.6 12.5 %collective-permute-start.5 = (f32[4,64,128]{2,1,0:T(8,128)S(1)}, f32[4,64,128]{2,1,0:T(8,128)S(1)}, u32[]{:S(2)}, u32[]{:S(2)}) collective-permute-start(f32[4,64,128]{2,1,0:T(8,128)S(1)} %get-tuple-element.23), channel_id=1, source_target_pairs={{0,2},{1,3},{2,0},{3,1},{4,6},{5,7},{6,4},{7,5},{8,10},{9,11},{10,... | collective-permute-start | bytes 393224 | tf_op jit(solution)/shard_map/ppermute | solution.py:343
  16.5 12.0 %collective-permute-start.6 = (f32[4,64,128]{2,1,0:T(8,128)S(1)}, f32[4,64,128]{2,1,0:T(8,128)S(1)}, u32[]{:S(2)}, u32[]{:S(2)}) collective-permute-start(f32[4,64,128]{2,1,0:T(8,128)S(1)} %get-tuple-element.26), channel_id=1, source_target_pairs={{0,3},{1,2},{2,1},{3,0},{4,7},{5,6},{6,5},{7,4},{8,11},{9,10},{10,... | collective-permute-start | bytes 393224 | tf_op jit(solution)/shard_map/ppermute | solution.py:343

commit v4 on v3

--- a/solution.py
+++ b/solution.py
@@ -227,15 +227,17 @@
     sweep(range(g), region, rows, a_ref, b_ref, acc_ref, out_ref)
 
 
-def slabs(rows, halo, source, out_hbm, sems):
+def slabs(rows, which, source, out_hbm, sems):
     top = rows - K
-    tiles = K // SUB
-    places = [] if halo else [((0, top), (0, K))]
-    for i in range(tiles):
-        edge = K - SUB * (i + 1)
-        lo, hi = (edge, K) if halo else (0, edge)
-        if hi > lo:
-            places.append(((top + SUB * i, SUB), (lo, hi - lo)))
+    if which == "top":
+        places = [((0, top), (0, K))]
+    else:
+        places = []
+        for i in range(K // SUB):
+            edge = K - SUB * (i + 1)
+            lo, hi = (edge, K) if which == "halo" else (0, edge)
+            if hi > lo:
+                places.append(((top + SUB * i, SUB), (lo, hi - lo)))
     copies = []
     for (row, n), (col, m) in places:
         at = (pl.ds(row, n), pl.ds(col * W, m * W))
@@ -243,33 +245,41 @@
     return copies
 
 
-def halo_sums(scale, groups, a_ref, b_ref, acc_ref, out_ref):
+def halo_factors(scale, groups, a_ref, b_ref):
     rows = a_ref.shape[2]
     g = 0
     for parts in groups:
         for r in range(parts[0].shape[0]):
             prepare(scale, parts, r, g, a_ref, b_ref, rows - K, rows - 2 * SUB)
             g += 1
-    sweep(range(g), "halo", rows, a_ref, b_ref, acc_ref, out_ref)
+    return range(g)
 
 
 def edge_kernel(scale, count, rows, acc_ref, *refs):
     groups = [refs[2 * i : 2 * i + 2] for i in range(count)]
     out_hbm, tail_ref, a_ref, b_ref, sems = refs[2 * count :]
-    copies = slabs(rows, False, acc_ref, out_hbm, sems)
+    copies = slabs(rows, "top", acc_ref, out_hbm, sems)
     for copy in copies:
         copy.start()
-    halo_sums(scale, groups, a_ref, b_ref, None, tail_ref)
+    records = halo_factors(scale, groups, a_ref, b_ref)
+    for i in range(STEPS):
+        step(STEPS - 1 + i, list(range(i, STEPS)), rows - K, records, a_ref, b_ref, None, tail_ref)
     for copy in copies:
         copy.wait()
 
 
-def finish_kernel(scale, rows, part_hbm, tail_ref, main_ref, halo_ref, out_hbm, sum_ref, a_ref, b_ref, sems):
-    halo_sums(scale, [[main_ref, halo_ref]], a_ref, b_ref, tail_ref, sum_ref)
-    copies = slabs(rows, True, sum_ref, out_hbm, sems)
-    for copy in copies:
+def finish_kernel(scale, count, rows, part_hbm, acc_ref, tail_ref, *refs):
+    groups = [refs[2 * i : 2 * i + 2] for i in range(count)]
+    out_hbm, sum_ref, a_ref, b_ref, sems = refs[2 * count :]
+    early = slabs(rows, "main", acc_ref, out_hbm, sems.at[0])
+    for copy in early:
         copy.start()
-    for copy in copies:
+    records = halo_factors(scale, groups, a_ref, b_ref)
+    late = slabs(rows, "halo", sum_ref, out_hbm, sems.at[1])
+    for i, copy in enumerate(late):
+        step(STEPS - 1 + i, list(range(i, STEPS)), rows - K, records, a_ref, b_ref, tail_ref, sum_ref)
+        copy.start()
+    for copy in early + late:
         copy.wait()
 
 
@@ -298,7 +308,6 @@
         in_specs=[VMEM] * (len(flat) + (acc is not None)),
         out_specs=VMEM,
         scratch_shapes=factors(records, rows),
-        input_output_aliases={0: 0} if acc is not None else {},
         compiler_params=PARAMS,
         cost_estimate=cost(records, rows),
         name="cross",
@@ -314,28 +323,29 @@
         out_shape=[out, out],
         in_specs=[VMEM] * (1 + len(flat)),
         out_specs=[HBM, VMEM],
-        scratch_shapes=factors(records, rows) + [pltpu.SemaphoreType.DMA((K // SUB,))],
+        scratch_shapes=factors(records, rows) + [pltpu.SemaphoreType.DMA((1,))],
         compiler_params=PARAMS,
-        cost_estimate=cost(records // 3, rows),
+        cost_estimate=cost(records // 2, rows),
         name="edge",
     )(acc, *flat)
 
 
-def finish(part, tail, main, halo, scale):
-    records, rows, _ = main.shape
+def finish(part, acc, tail, groups, rows, scale):
+    records = sum(g[0].shape[0] for g in groups)
+    flat = [p for g in groups for p in g]
     return pl.pallas_call(
-        functools.partial(finish_kernel, scale, rows),
+        functools.partial(finish_kernel, scale, len(groups), rows),
         out_shape=jax.ShapeDtypeStruct((rows, K * W), jnp.float32),
-        in_specs=[HBM] + [VMEM] * 3,
+        in_specs=[HBM] + [VMEM] * (2 + len(flat)),
         out_specs=HBM,
         scratch_shapes=[pltpu.VMEM((rows, K * W), jnp.float32)]
         + factors(records, rows)
-        + [pltpu.SemaphoreType.DMA((K // SUB,))],
+        + [pltpu.SemaphoreType.DMA((2, K // SUB))],
         input_output_aliases={0: 0},
         compiler_params=PARAMS,
-        cost_estimate=cost(records // 3, rows),
+        cost_estimate=cost(records // 2, rows),
         name="finish",
-    )(part, tail, main, halo)
+    )(part, acc, tail, *flat)
 
 
 def send(shard, by):
@@ -365,17 +375,19 @@
     def block(by):
         return (lambda me: lax.bitwise_xor(me, by) * rows, rows)
 
-    far, one, two, own, head = whiten(strain, [block(3), block(1), block(2), block(0)], pair)
+    one, two, head_a = whiten(strain, [block(1), block(2)], pair)
+    one_in, two_in = send(one, 1), send(two, 2)
+    far, own, head_b = whiten(strain, [block(3), block(0)], pair)
+    far_in = send(far, 3)
+    me = lax.axis_index("rec")
+    head = jnp.where((me == 1) | (me == 2), head_a, head_b)
     below = shifted(head, "chan", -1)
-    far_in, one_in, two_in = send(far, 3), send(one, 1), send(two, 2)
     own_halo, one_halo, two_halo, far_halo = halos([own, one, two, far], below)
     one_halo_in, two_halo_in, far_halo_in = send(one_halo, 1), send(two_halo, 2), send(far_halo, 3)
-    acc = cross([[own], [far_in]], "main", rows, scale)
-    acc = cross([[one_in], [two_in]], "main", rows, scale, acc)
-    part, tail = edge(
-        acc, [[own, own_halo], [one_in, one_halo_in], [two_in, two_halo_in]], rows, scale
-    )
-    return finish(part, tail, far_in, far_halo_in, scale)
+    acc = cross([[own]], "main", rows, scale)
+    acc = cross([[one_in], [two_in], [far_in]], "main", rows, scale, acc)
+    part, tail = edge(acc, [[own, own_halo], [one_in, one_halo_in]], rows, scale)
+    return finish(part, acc, tail, [[two_in, two_halo_in], [far_in, far_halo_in]], rows, scale)
 
 
 def general(strain, rows, scale):

time: 30.8 us -> 30 us (0.974)
  the two profiles are of different devices: /device:TPU:0 before, /device:TPU:1 now
where the time goes in v4:
time: 30 us; the launch traced here: 29.9 us
  Pallas kernels  17.3 us (58%)
  starting transfers between devices  9.29 us (31%)
  waiting for transfers between devices  2.99 us (10%)
    pallas_call x2, Pallas kernels, whiten(): pl.pallas_call(functools.partial(whiten_kernel, jobs, pair), out_shape=ou...  6.61 us
    pallas_call x2, Pallas kernels, cross(): pl.pallas_call(functools.partial(cross_kernel, scale, [len(g) for g in gr...  6.28 us
    ppermute x6, starting transfers between devices, send(): return lax.ppermute(shard, 'rec', [(i, i ^ by) for i in range(size)])  6.15 us
    ppermute x1, starting transfers between devices, shifted(): return lax.ppermute(shard, axis, pairs)  3.14 us
    ppermute x1, waiting for transfers between devices, shifted(): return lax.ppermute(shard, axis, pairs)  2.98 us
    pallas_call x1, Pallas kernels, finish(): pl.pallas_call(functools.partial(finish_kernel, scale, len(groups), rows)...  2.55 us
    pallas_call x1, Pallas kernels, edge(): pl.pallas_call(functools.partial(edge_kernel, scale, len(groups), rows),...  1.61 us
  transfers between devices with their start and end apart: 7, of which 1 were waited for; matrix products, arithmetic and copies ran while one was open for 0% of the time, Pallas kernels for 38%

profile of v4, /device:TPU:1, one launch (start us, length us, event | category | flops | bytes accessed | tf_op | source)
XLA Modules:
  0.0 29.9 jit_solution(776788139669523678)
XLA Ops:
  0.0 3.3 %whiten.3 = (f32[4,128,128]{2,1,0:T(8,128)S(1)}, f32[4,128,128]{2,1,0:T(8,128)S(1)}, f32[4,64,128]{2,1,0:T(8,128)S(1)}) custom-call(bf16[4,512,2048]{2,1,0:T(8,128)(2,1)} %strain_hbm.3), custom_call_target="tpu_custom_call" | custom-call | flops 536870912 | bytes 4194304 | tf_op jit(solution)/shard_map/whiten/pallas_call | solution.py:76
  3.3 2.1 %collective-permute-start = (f32[4,128,128]{2,1,0:T(8,128)S(1)}, f32[4,128,128]{2,1,0:T(8,128)S(1)}, u32[]{:S(2)}, u32[]{:S(2)}) collective-permute-start(f32[4,128,128]{2,1,0:T(8,128)S(1)} %get-tuple-element.18.refs_1_), channel_id=1, source_target_pairs={{0,1},{1,0},{2,3},{3,2},{4,5},{5,4},{6,7},{7,6},{8,9},{9,8},{10,11... | collective-permute-start | bytes 786440 | tf_op jit(solution)/shard_map/ppermute | solution.py:353
  5.4 1.2 %collective-permute-start.1 = (f32[4,128,128]{2,1,0:T(8,128)S(1)}, f32[4,128,128]{2,1,0:T(8,128)S(1)}, u32[]{:S(2)}, u32[]{:S(2)}) collective-permute-start(f32[4,128,128]{2,1,0:T(8,128)S(1)} %get-tuple-element.19.refs_2_), channel_id=1, source_target_pairs={{0,2},{1,3},{2,0},{3,1},{4,6},{5,7},{6,4},{7,5},{8,10},{9,11},{10,... | collective-permute-start | bytes 786440 | tf_op jit(solution)/shard_map/ppermute | solution.py:353
  6.7 3.3 %whiten.2 = (f32[4,128,128]{2,1,0:T(8,128)S(1)}, f32[4,128,128]{2,1,0:T(8,128)S(1)}, f32[4,64,128]{2,1,0:T(8,128)S(1)}) custom-call(bf16[4,512,2048]{2,1,0:T(8,128)(2,1)} %strain_hbm.3), custom_call_target="tpu_custom_call" | custom-call | flops 536870912 | bytes 4194304 | tf_op jit(solution)/shard_map/whiten/pallas_call | solution.py:76
  10.0 0.1 collective-permute-start.2
  10.1 3.1 %collective-permute-start.3 = (f32[4,64,128]{2,1,0:T(8,128)S(1)}, f32[4,64,128]{2,1,0:T(8,128)S(1)}, u32[]{:S(2)}, u32[]{:S(2)}) collective-permute-start(f32[4,64,128]{2,1,0:T(8,128)S(1)} %broadcast_select_fusion), channel_id=1, source_target_pairs={{4,0},{8,4},{12,8},{16,12},{20,16},{24,20},{28,24},{5,1},{9,5},{13... | collective-permute-start | bytes 393224 | tf_op jit(solution)/shard_map/ppermute | solution.py:359
  13.2 1.6 %cross.2.refs_0_ = f32[128,8192]{1,0:T(8,128)S(1)} custom-call(f32[4,128,128]{2,1,0:T(8,128)S(1)} %get-tuple-element.17.refs_0_), custom_call_target="tpu_custom_call" | custom-call | flops 2097152000 | tf_op jit(solution)/shard_map/cross/pallas_call | solution.py:303
  14.8 3.0 %collective-permute-done.3.refs_4_ = f32[4,64,128]{2,1,0:T(8,128)S(1)} collective-permute-done((f32[4,64,128]{2,1,0:T(8,128)S(1)}, f32[4,64,128]{2,1,0:T(8,128)S(1)}, u32[]{:S(2)}, u32[]{:S(2)}) %collective-permute-start.3) | collective-permute-done | bytes 131104 | tf_op jit(solution)/shard_map/ppermute | solution.py:359
  17.8 0.3 halo.1
  18.1 1.3 %collective-permute-start.4 = (f32[4,64,128]{2,1,0:T(8,128)S(1)}, f32[4,64,128]{2,1,0:T(8,128)S(1)}, u32[]{:S(2)}, u32[]{:S(2)}) collective-permute-start(f32[4,64,128]{2,1,0:T(8,128)S(1)} %get-tuple-element.24), channel_id=1, source_target_pairs={{0,1},{1,0},{2,3},{3,2},{4,5},{5,4},{6,7},{7,6},{8,9},{9,8},{10,11... | collective-permute-start | bytes 393224 | tf_op jit(solution)/shard_map/ppermute | solution.py:353
  19.4 1.2 %collective-permute-start.5 = (f32[4,64,128]{2,1,0:T(8,128)S(1)}, f32[4,64,128]{2,1,0:T(8,128)S(1)}, u32[]{:S(2)}, u32[]{:S(2)}) collective-permute-start(f32[4,64,128]{2,1,0:T(8,128)S(1)} %get-tuple-element.27), channel_id=1, source_target_pairs={{0,2},{1,3},{2,0},{3,1},{4,6},{5,7},{6,4},{7,5},{8,10},{9,11},{10,... | collective-permute-start | bytes 393224 | tf_op jit(solution)/shard_map/ppermute | solution.py:353
  20.6 0.0 collective-permute-done.refs_1_.refs_2_
  20.6 0.2 collective-permute-start.6
  20.8 0.0 collective-permute-done.1.refs_2_.refs_0_
  20.8 0.0 collective-permute-done.2.refs_3_.refs_2_
  20.8 4.7 %cross.3.acc_ref = f32[128,8192]{1,0:T(8,128)S(1)} custom-call(f32[128,8192]{1,0:T(8,128)S(1)} %cross.2.refs_0_, f32[4,128,128]{2,1,0:T(8,128)S(1)} %collective-permute-done.refs_1_.refs_2_, f32[4,128,128]{2,1,0:T(8,128)S(1)} %collective-permute-done.1.refs_2_.refs_0_, f32[4,128,128]{2,1,0:T(8,128)S(1)} %collective-permute-done.2.refs_3_.refs_2_), custom_call_target="tpu_custom_call" | custom-call | flops 6291456000 | tf_op jit(solution)/shard_map/cross/pallas_call | solution.py:303
  25.5 0.0 collective-permute-done.4.refs_3_
  25.5 1.6 %edge.1 = (f32[128,8192]{1,0:T(8,128)}, f32[128,8192]{1,0:T(8,128)S(1)}) custom-call(f32[128,8192]{1,0:T(8,128)S(1)} %cross.3.acc_ref, f32[4,128,128]{2,1,0:T(8,128)S(1)} %get-tuple-element.17.refs_0_, f32[4,64,128]{2,1,0:T(8,128)S(1)} %get-tuple-element.23.refs_1_, f32[4,128,128]{2,1,0:T(8,128)S(1)} %collective-permute-done.refs_1_.refs_2_, ...), custom_call_target="tpu_custom_call" | custom-call | flops 2097152000 | tf_op jit(solution)/shard_map/edge/pallas_call | solution.py:321
  27.1 0.0 collective-permute-done.5.refs_1_
  27.2 0.0 collective-permute-done.6.refs_3_
  27.2 2.6 %finish.1 = f32[128,8192]{1,0:T(8,128)} custom-call(f32[128,8192]{1,0:T(8,128)} %get-tuple-element.25.part_hbm, f32[128,8192]{1,0:T(8,128)S(1)} %cross.3.acc_ref, f32[128,8192]{1,0:T(8,128)S(1)} %get-tuple-element.26.tail_ref, f32[4,128,128]{2,1,0:T(8,128)S(1)} %collective-permute-done.1.refs_2_.refs_0_, ...), custom_call_target="tpu_custom_call", output_to_operand_aliasing={{}: (0, {})} | custom-call | flops 2097152000 | tf_op jit(solution)/shard_map/finish/pallas_call | solution.py:336
  (1 shorter events, 0.0 us)
Async XLA Ops:
  3.3 17.3 %collective-permute-start = (f32[4,128,128]{2,1,0:T(8,128)S(1)}, f32[4,128,128]{2,1,0:T(8,128)S(1)}, u32[]{:S(2)}, u32[]{:S(2)}) collective-permute-start(f32[4,128,128]{2,1,0:T(8,128)S(1)} %get-tuple-element.18.refs_1_), channel_id=1, source_target_pairs={{0,1},{1,0},{2,3},{3,2},{4,5},{5,4},{6,7},{7,6},{8,9},{9,8},{10,11... | collective-permute-start | bytes 786440 | tf_op jit(solution)/shard_map/ppermute | solution.py:353
  5.4 15.4 %collective-permute-start.1 = (f32[4,128,128]{2,1,0:T(8,128)S(1)}, f32[4,128,128]{2,1,0:T(8,128)S(1)}, u32[]{:S(2)}, u32[]{:S(2)}) collective-permute-start(f32[4,128,128]{2,1,0:T(8,128)S(1)} %get-tuple-element.19.refs_2_), channel_id=1, source_target_pairs={{0,2},{1,3},{2,0},{3,1},{4,6},{5,7},{6,4},{7,5},{8,10},{9,11},{10,... | collective-permute-start | bytes 786440 | tf_op jit(solution)/shard_map/ppermute | solution.py:353
  10.0 10.8 %collective-permute-start.2 = (f32[4,128,128]{2,1,0:T(8,128)S(1)}, f32[4,128,128]{2,1,0:T(8,128)S(1)}, u32[]{:S(2)}, u32[]{:S(2)}) collective-permute-start(f32[4,128,128]{2,1,0:T(8,128)S(1)} %get-tuple-element.20.refs_3_), channel_id=1, source_target_pairs={{0,3},{1,2},{2,1},{3,0},{4,7},{5,6},{6,5},{7,4},{8,11},{9,10},{10,... | collective-permute-start | bytes 786440 | tf_op jit(solution)/shard_map/ppermute | solution.py:353
  10.1 7.7 %collective-permute-start.3 = (f32[4,64,128]{2,1,0:T(8,128)S(1)}, f32[4,64,128]{2,1,0:T(8,128)S(1)}, u32[]{:S(2)}, u32[]{:S(2)}) collective-permute-start(f32[4,64,128]{2,1,0:T(8,128)S(1)} %broadcast_select_fusion), channel_id=1, source_target_pairs={{4,0},{8,4},{12,8},{16,12},{20,16},{24,20},{28,24},{5,1},{9,5},{13... | collective-permute-start | bytes 393224 | tf_op jit(solution)/shard_map/ppermute | solution.py:359
  18.1 7.4 %collective-permute-start.4 = (f32[4,64,128]{2,1,0:T(8,128)S(1)}, f32[4,64,128]{2,1,0:T(8,128)S(1)}, u32[]{:S(2)}, u32[]{:S(2)}) collective-permute-start(f32[4,64,128]{2,1,0:T(8,128)S(1)} %get-tuple-element.24), channel_id=1, source_target_pairs={{0,1},{1,0},{2,3},{3,2},{4,5},{5,4},{6,7},{7,6},{8,9},{9,8},{10,11... | collective-permute-start | bytes 393224 | tf_op jit(solution)/shard_map/ppermute | solution.py:353
  19.4 7.8 %collective-permute-start.5 = (f32[4,64,128]{2,1,0:T(8,128)S(1)}, f32[4,64,128]{2,1,0:T(8,128)S(1)}, u32[]{:S(2)}, u32[]{:S(2)}) collective-permute-start(f32[4,64,128]{2,1,0:T(8,128)S(1)} %get-tuple-element.27), channel_id=1, source_target_pairs={{0,2},{1,3},{2,0},{3,1},{4,6},{5,7},{6,4},{7,5},{8,10},{9,11},{10,... | collective-permute-start | bytes 393224 | tf_op jit(solution)/shard_map/ppermute | solution.py:353
  20.6 6.6 %collective-permute-start.6 = (f32[4,64,128]{2,1,0:T(8,128)S(1)}, f32[4,64,128]{2,1,0:T(8,128)S(1)}, u32[]{:S(2)}, u32[]{:S(2)}) collective-permute-start(f32[4,64,128]{2,1,0:T(8,128)S(1)} %get-tuple-element.28), channel_id=1, source_target_pairs={{0,3},{1,2},{2,1},{3,0},{4,7},{5,6},{6,5},{7,4},{8,11},{9,10},{10,... | collective-permute-start | bytes 393224 | tf_op jit(solution)/shard_map/ppermute | solution.py:353

commit v5 on v4

--- a/solution.py
+++ b/solution.py
@@ -38,7 +38,7 @@
 
 
 def whiten_kernel(jobs, pair, strain_hbm, *refs):
-    outs, head_ref, refs = refs[: len(jobs)], refs[len(jobs)], refs[len(jobs) + 1 :]
+    outs, refs = refs[: len(jobs)], refs[len(jobs) :]
     table_ref, sems, bufs = refs[0], refs[1], refs[2:]
     me = lax.axis_index("rec")
     copies = []
@@ -63,16 +63,11 @@
             power = jnp.sum(spec * spec, axis=-1, keepdims=True) * (1.0 / F)
             out[r : r + pair] = (spec * lax.rsqrt(power + 1e-06)).reshape(pair, rows, W)
 
-        @pl.when(start(me) == 0)
-        def _():
-            head_ref[...] = out[:, :K]
-
 
 def whiten(strain, jobs, pair):
     records = strain.shape[0]
     total = sum(rows for _, rows in jobs)
     outs = [jax.ShapeDtypeStruct((records, rows, W), jnp.float32) for _, rows in jobs]
-    outs.append(jax.ShapeDtypeStruct((records, K, W), jnp.float32))
     return pl.pallas_call(
         functools.partial(whiten_kernel, jobs, pair),
         out_shape=outs,
@@ -375,17 +370,16 @@
     def block(by):
         return (lambda me: lax.bitwise_xor(me, by) * rows, rows)
 
-    one, two, head_a = whiten(strain, [block(1), block(2)], pair)
+    far, head = whiten(strain, [block(3), (lambda me: 0 * me, K)], pair)
+    below = shifted(head, "chan", -1)
+    far_in = send(far, 3)
+    one, two = whiten(strain, [block(1), block(2)], pair)
+    (own,) = whiten(strain, [block(0)], pair)
     one_in, two_in = send(one, 1), send(two, 2)
-    far, own, head_b = whiten(strain, [block(3), block(0)], pair)
-    far_in = send(far, 3)
-    me = lax.axis_index("rec")
-    head = jnp.where((me == 1) | (me == 2), head_a, head_b)
-    below = shifted(head, "chan", -1)
     own_halo, one_halo, two_halo, far_halo = halos([own, one, two, far], below)
     one_halo_in, two_halo_in, far_halo_in = send(one_halo, 1), send(two_halo, 2), send(far_halo, 3)
-    acc = cross([[own]], "main", rows, scale)
-    acc = cross([[one_in], [two_in], [far_in]], "main", rows, scale, acc)
+    acc = cross([[own], [far_in]], "main", rows, scale)
+    acc = cross([[one_in], [two_in]], "main", rows, scale, acc)
     part, tail = edge(acc, [[own, own_halo], [one_in, one_halo_in]], rows, scale)
     return finish(part, acc, tail, [[two_in, two_halo_in], [far_in, far_halo_in]], rows, scale)
 
@@ -394,8 +388,8 @@
     records, channels, _ = strain.shape
     size = lax.axis_size("rec")
     me = lax.axis_index("rec")
-    spectra, head = whiten(strain, [(lambda me: 0 * me, channels)], 1)
-    below = shifted(head, "chan", -1)
+    (spectra,) = whiten(strain, [(lambda me: 0 * me, channels)], 1)
+    below = shifted(spectra[:, :K], "chan", -1)
     extended = jnp.concatenate([spectra, below], axis=1)
     acc = None
     for by in range(size):

time: 30 us -> 29.7 us (0.990)
  the two profiles are of different devices: /device:TPU:1 before, /device:TPU:0 now
where the time goes in v5:
time: 29.7 us; the launch traced here: 29.6 us
  Pallas kernels  19 us (64%)
  starting transfers between devices  9.45 us (32%)
  waiting for transfers between devices  0.86 us (3%)
    pallas_call x3, Pallas kernels, whiten(): pl.pallas_call(functools.partial(whiten_kernel, jobs, pair), out_shape=ou...  8.61 us
    ppermute x6, starting transfers between devices, send(): return lax.ppermute(shard, 'rec', [(i, i ^ by) for i in range(size)])  8.17 us
    pallas_call x2, Pallas kernels, cross(): pl.pallas_call(functools.partial(cross_kernel, scale, [len(g) for g in gr...  5.98 us
    pallas_call x1, Pallas kernels, finish(): pl.pallas_call(functools.partial(finish_kernel, scale, len(groups), rows)...  2.55 us
    pallas_call x1, Pallas kernels, edge(): pl.pallas_call(functools.partial(edge_kernel, scale, len(groups), rows),...  1.61 us
    ppermute x1, starting transfers between devices, shifted(): return lax.ppermute(shard, axis, pairs)  1.28 us
    ppermute x6, waiting for transfers between devices, send(): return lax.ppermute(shard, 'rec', [(i, i ^ by) for i in range(size)])  0.86 us
  transfers between devices with their start and end apart: 7, of which 1 were waited for; matrix products, arithmetic and copies ran while one was open for 0% of the time, Pallas kernels for 45%

profile of v5, /device:TPU:0, one launch (start us, length us, event | category | flops | bytes accessed | tf_op | source)
XLA Modules:
  0.0 29.6 jit_solution(10641193371174050889)
XLA Ops:
  0.0 3.0 %whiten.4 = (f32[4,128,128]{2,1,0:T(8,128)S(1)}, f32[4,64,128]{2,1,0:T(8,128)S(1)}) custom-call(bf16[4,512,2048]{2,1,0:T(8,128)(2,1)} %strain_hbm.5), custom_call_target="tpu_custom_call" | custom-call | flops 402653184 | bytes 3145728 | tf_op jit(solution)/shard_map/whiten/pallas_call | solution.py:71
  3.0 4.0 %collective-permute-start = (f32[4,128,128]{2,1,0:T(8,128)S(1)}, f32[4,128,128]{2,1,0:T(8,128)S(1)}, u32[]{:S(2)}, u32[]{:S(2)}) collective-permute-start(f32[4,128,128]{2,1,0:T(8,128)S(1)} %get-tuple-element.15.refs_3_), channel_id=1, source_target_pairs={{0,3},{1,2},{2,1},{3,0},{4,7},{5,6},{6,5},{7,4},{8,11},{9,10},{10,... | collective-permute-start | bytes 786440 | tf_op jit(solution)/shard_map/ppermute | solution.py:348
  7.0 1.3 %collective-permute-start.3 = (f32[4,64,128]{2,1,0:T(8,128)S(1)}, f32[4,64,128]{2,1,0:T(8,128)S(1)}, u32[]{:S(2)}, u32[]{:S(2)}) collective-permute-start(f32[4,64,128]{2,1,0:T(8,128)S(1)} %get-tuple-element.18), channel_id=1, source_target_pairs={{4,0},{8,4},{12,8},{16,12},{20,16},{24,20},{28,24},{5,1},{9,5},{13... | collective-permute-start | bytes 393224 | tf_op jit(solution)/shard_map/ppermute | solution.py:354
  8.3 3.3 %whiten.5 = (f32[4,128,128]{2,1,0:T(8,128)S(1)}, f32[4,128,128]{2,1,0:T(8,128)S(1)}) custom-call(bf16[4,512,2048]{2,1,0:T(8,128)(2,1)} %strain_hbm.5), custom_call_target="tpu_custom_call" | custom-call | flops 536870912 | bytes 4194304 | tf_op jit(solution)/shard_map/whiten/pallas_call | solution.py:71
  11.6 0.6 %collective-permute-start.1 = (f32[4,128,128]{2,1,0:T(8,128)S(1)}, f32[4,128,128]{2,1,0:T(8,128)S(1)}, u32[]{:S(2)}, u32[]{:S(2)}) collective-permute-start(f32[4,128,128]{2,1,0:T(8,128)S(1)} %get-tuple-element.16.refs_1_), channel_id=1, source_target_pairs={{0,1},{1,0},{2,3},{3,2},{4,5},{5,4},{6,7},{7,6},{8,9},{9,8},{10,11... | collective-permute-start | bytes 786440 | tf_op jit(solution)/shard_map/ppermute | solution.py:348
  12.2 0.1 collective-permute-start.2
  12.3 2.3 %whiten.3.refs_0_ = f32[4,128,128]{2,1,0:T(8,128)S(1)} custom-call(bf16[4,512,2048]{2,1,0:T(8,128)(2,1)} %strain_hbm.5), custom_call_target="tpu_custom_call" | custom-call | flops 268435456 | bytes 2097152 | tf_op jit(solution)/shard_map/whiten/pallas_call | solution.py:71
  14.5 0.0 collective-permute-done.3.refs_4_
  14.5 0.3 halo.1
  14.8 2.0 %collective-permute-start.4 = (f32[4,64,128]{2,1,0:T(8,128)S(1)}, f32[4,64,128]{2,1,0:T(8,128)S(1)}, u32[]{:S(2)}, u32[]{:S(2)}) collective-permute-start(f32[4,64,128]{2,1,0:T(8,128)S(1)} %get-tuple-element.20), channel_id=1, source_target_pairs={{0,1},{1,0},{2,3},{3,2},{4,5},{5,4},{6,7},{7,6},{8,9},{9,8},{10,11... | collective-permute-start | bytes 393224 | tf_op jit(solution)/shard_map/ppermute | solution.py:348
  16.9 1.5 %collective-permute-start.5 = (f32[4,64,128]{2,1,0:T(8,128)S(1)}, f32[4,64,128]{2,1,0:T(8,128)S(1)}, u32[]{:S(2)}, u32[]{:S(2)}) collective-permute-start(f32[4,64,128]{2,1,0:T(8,128)S(1)} %get-tuple-element.23), channel_id=1, source_target_pairs={{0,2},{1,3},{2,0},{3,1},{4,6},{5,7},{6,4},{7,5},{8,10},{9,11},{10,... | collective-permute-start | bytes 393224 | tf_op jit(solution)/shard_map/ppermute | solution.py:348
  18.4 0.0 collective-permute-done.refs_1_.refs_2_
  18.4 0.0 collective-permute-start.6
  18.4 2.9 %cross.2.refs_0_ = f32[128,8192]{1,0:T(8,128)S(1)} custom-call(f32[4,128,128]{2,1,0:T(8,128)S(1)} %whiten.3.refs_0_, f32[4,128,128]{2,1,0:T(8,128)S(1)} %collective-permute-done.refs_1_.refs_2_), custom_call_target="tpu_custom_call" | custom-call | flops 4194304000 | tf_op jit(solution)/shard_map/cross/pallas_call | solution.py:298
  21.3 0.0 collective-permute-done.1.refs_1_.refs_2_
  21.4 0.0 collective-permute-done.2.refs_2_.refs_0_
  21.4 3.0 %cross.3.acc_ref = f32[128,8192]{1,0:T(8,128)S(1)} custom-call(f32[128,8192]{1,0:T(8,128)S(1)} %cross.2.refs_0_, f32[4,128,128]{2,1,0:T(8,128)S(1)} %collective-permute-done.1.refs_1_.refs_2_, f32[4,128,128]{2,1,0:T(8,128)S(1)} %collective-permute-done.2.refs_2_.refs_0_), custom_call_target="tpu_custom_call" | custom-call | flops 4194304000 | tf_op jit(solution)/shard_map/cross/pallas_call | solution.py:298
  24.4 0.0 collective-permute-done.4.refs_3_
  24.4 1.6 %edge.1 = (f32[128,8192]{1,0:T(8,128)}, f32[128,8192]{1,0:T(8,128)S(1)}) custom-call(f32[128,8192]{1,0:T(8,128)S(1)} %cross.3.acc_ref, f32[4,128,128]{2,1,0:T(8,128)S(1)} %whiten.3.refs_0_, f32[4,64,128]{2,1,0:T(8,128)S(1)} %get-tuple-element.19.refs_1_, f32[4,128,128]{2,1,0:T(8,128)S(1)} %collective-permute-done.1.refs_1_.refs_2_, ...), custom_call_target="tpu_custom_call" | custom-call | flops 2097152000 | tf_op jit(solution)/shard_map/edge/pallas_call | solution.py:316
  26.1 0.8 %collective-permute-done.5.refs_1_ = f32[4,64,128]{2,1,0:T(8,128)S(1)} collective-permute-done((f32[4,64,128]{2,1,0:T(8,128)S(1)}, f32[4,64,128]{2,1,0:T(8,128)S(1)}, u32[]{:S(2)}, u32[]{:S(2)}) %collective-permute-start.5) | collective-permute-done | bytes 131104 | tf_op jit(solution)/shard_map/ppermute | solution.py:348
  26.9 0.0 collective-permute-done.6.refs_3_
  26.9 2.5 %finish.1 = f32[128,8192]{1,0:T(8,128)} custom-call(f32[128,8192]{1,0:T(8,128)} %get-tuple-element.21.part_hbm, f32[128,8192]{1,0:T(8,128)S(1)} %cross.3.acc_ref, f32[128,8192]{1,0:T(8,128)S(1)} %get-tuple-element.22.tail_ref, f32[4,128,128]{2,1,0:T(8,128)S(1)} %collective-permute-done.2.refs_2_.refs_0_, ...), custom_call_target="tpu_custom_call", output_to_operand_aliasing={{}: (0, {})} | custom-call | flops 2097152000 | tf_op jit(solution)/shard_map/finish/pallas_call | solution.py:331
Async XLA Ops:
  3.0 15.3 %collective-permute-start = (f32[4,128,128]{2,1,0:T(8,128)S(1)}, f32[4,128,128]{2,1,0:T(8,128)S(1)}, u32[]{:S(2)}, u32[]{:S(2)}) collective-permute-start(f32[4,128,128]{2,1,0:T(8,128)S(1)} %get-tuple-element.15.refs_3_), channel_id=1, source_target_pairs={{0,3},{1,2},{2,1},{3,0},{4,7},{5,6},{6,5},{7,4},{8,11},{9,10},{10,... | collective-permute-start | bytes 786440 | tf_op jit(solution)/shard_map/ppermute | solution.py:348
  7.0 7.5 %collective-permute-start.3 = (f32[4,64,128]{2,1,0:T(8,128)S(1)}, f32[4,64,128]{2,1,0:T(8,128)S(1)}, u32[]{:S(2)}, u32[]{:S(2)}) collective-permute-start(f32[4,64,128]{2,1,0:T(8,128)S(1)} %get-tuple-element.18), channel_id=1, source_target_pairs={{4,0},{8,4},{12,8},{16,12},{20,16},{24,20},{28,24},{5,1},{9,5},{13... | collective-permute-start | bytes 393224 | tf_op jit(solution)/shard_map/ppermute | solution.py:354
  11.6 9.7 %collective-permute-start.1 = (f32[4,128,128]{2,1,0:T(8,128)S(1)}, f32[4,128,128]{2,1,0:T(8,128)S(1)}, u32[]{:S(2)}, u32[]{:S(2)}) collective-permute-start(f32[4,128,128]{2,1,0:T(8,128)S(1)} %get-tuple-element.16.refs_1_), channel_id=1, source_target_pairs={{0,1},{1,0},{2,3},{3,2},{4,5},{5,4},{6,7},{7,6},{8,9},{9,8},{10,11... | collective-permute-start | bytes 786440 | tf_op jit(solution)/shard_map/ppermute | solution.py:348
  12.2 9.2 %collective-permute-start.2 = (f32[4,128,128]{2,1,0:T(8,128)S(1)}, f32[4,128,128]{2,1,0:T(8,128)S(1)}, u32[]{:S(2)}, u32[]{:S(2)}) collective-permute-start(f32[4,128,128]{2,1,0:T(8,128)S(1)} %get-tuple-element.17.refs_2_), channel_id=1, source_target_pairs={{0,2},{1,3},{2,0},{3,1},{4,6},{5,7},{6,4},{7,5},{8,10},{9,11},{10,... | collective-permute-start | bytes 786440 | tf_op jit(solution)/shard_map/ppermute | solution.py:348
  14.8 9.6 %collective-permute-start.4 = (f32[4,64,128]{2,1,0:T(8,128)S(1)}, f32[4,64,128]{2,1,0:T(8,128)S(1)}, u32[]{:S(2)}, u32[]{:S(2)}) collective-permute-start(f32[4,64,128]{2,1,0:T(8,128)S(1)} %get-tuple-element.20), channel_id=1, source_target_pairs={{0,1},{1,0},{2,3},{3,2},{4,5},{5,4},{6,7},{7,6},{8,9},{9,8},{10,11... | collective-permute-start | bytes 393224 | tf_op jit(solution)/shard_map/ppermute | solution.py:348
  16.9 10.0 %collective-permute-start.5 = (f32[4,64,128]{2,1,0:T(8,128)S(1)}, f32[4,64,128]{2,1,0:T(8,128)S(1)}, u32[]{:S(2)}, u32[]{:S(2)}) collective-permute-start(f32[4,64,128]{2,1,0:T(8,128)S(1)} %get-tuple-element.23), channel_id=1, source_target_pairs={{0,2},{1,3},{2,0},{3,1},{4,6},{5,7},{6,4},{7,5},{8,10},{9,11},{10,... | collective-permute-start | bytes 393224 | tf_op jit(solution)/shard_map/ppermute | solution.py:348
  18.4 8.5 %collective-permute-start.6 = (f32[4,64,128]{2,1,0:T(8,128)S(1)}, f32[4,64,128]{2,1,0:T(8,128)S(1)}, u32[]{:S(2)}, u32[]{:S(2)}) collective-permute-start(f32[4,64,128]{2,1,0:T(8,128)S(1)} %get-tuple-element.24), channel_id=1, source_target_pairs={{0,3},{1,2},{2,1},{3,0},{4,7},{5,6},{6,5},{7,4},{8,11},{9,10},{10,... | collective-permute-start | bytes 393224 | tf_op jit(solution)/shard_map/ppermute | solution.py:348
